TPU v7x, 512 devices: a whole 4x4x16 slice. The times are simulated.
512 devices in a mesh: dp: 32 (over z, x_hi), row: 8 (over y, core), col: 2 (over x_lo).
Axes of the slice: x: 4 (x_hi: 2, x_lo: 2; x = x_hi * 2 + x_lo), y: 4, z: 16, core: 2. Of those that a mesh axis runs over, the one named last changes fastest.
Arguments:
- counts: int32 [24576, 16384], P('dp', ('row', 'col')), may hold values from 0 to 32, as said below
- coef: float32 [16384, 512], P(('row', 'col'), 'dp'), may hold values from -0.3 to 1.5, as said below
Outputs:
- new_coef: float32 [16384, 512], P(('row', 'col'), 'dp')
- objective: float32 [], replicated
Inputs may be any that keep to these rules, and one draw needn't show every extreme that they name: Whole counts. `coef`: diagonal positions hold 0.5 to 1.5.
All inputs are finite; a program needn't handle non-finite values.
Results may differ from a plain program's by a relative error of at most 0.006.
Values may be sent and summed in bfloat16 or wider, within the bound.
No kernel may reach another device: no remote copies, remote signals or barrier semaphores. Data moves between devices by JAX's collectives and lax.ppermute only.
A program may use at most 64 MiB of HBM per device.

v0:
```python
import jax
import jax.numpy as jnp
from jax import lax
from jax.sharding import PartitionSpec as P

STEP = 0.5
PENALTY = 0.05
SCALE = 10000.0


def per_device(counts, coef):
    cells = counts.shape[0]
    genes_loc = counts.shape[1]
    cols_loc = coef.shape[1]
    n_dp = lax.axis_size("dp")
    n_tile = lax.axis_size("row") * lax.axis_size("col")
    band = cols_loc * n_dp
    total = float(cells * n_dp)
    tile = lax.axis_index("row") * lax.axis_size("col") + lax.axis_index("col")
    part_idx = lax.axis_index("dp")
    counts_f = counts.astype(jnp.float32)
    library = lax.psum(jnp.sum(counts_f, axis=1), ("row", "col"))
    expression = jnp.log1p(SCALE * counts_f / (library[:, None] + 1.0))
    means = lax.psum(jnp.sum(expression, axis=0), "dp") / total
    centered = (expression - means).astype(jnp.bfloat16)
    coef_low = coef.astype(jnp.bfloat16)
    partial_proj = jnp.dot(
        centered,
        lax.all_gather(coef_low, "dp", axis=1, tiled=True),
        preferred_element_type=jnp.float32,
    )
    projection = lax.psum(partial_proj, ("row", "col"))
    projection_low = projection.astype(jnp.bfloat16)
    quad_term = jnp.sum(projection * projection) / n_tile
    covar_rows = lax.psum_scatter(
        lax.dot_general(
            projection_low, centered, (((0,), (0,)), ((), ())), preferred_element_type=jnp.float32
        ).astype(jnp.bfloat16),
        "dp",
        scatter_dimension=0,
        tiled=True,
    ).astype(jnp.float32)
    covar_coef = covar_rows.T / total
    rows_id = lax.broadcasted_iota(jnp.int32, (genes_loc, cols_loc), 0) + tile * genes_loc
    cols_id = lax.broadcasted_iota(jnp.int32, (genes_loc, cols_loc), 1) + part_idx * cols_loc
    on_diag = rows_id == cols_id
    safe = jnp.where(on_diag, coef, 1.0)
    inverse = jnp.where(on_diag, 1.0 / safe, 0.0)
    gradient = covar_coef - inverse
    stepped = coef - STEP * gradient
    limit = STEP * PENALTY
    shrunk = jnp.where(on_diag, stepped, stepped - jnp.clip(stepped, -limit, limit))
    top = shrunk[:band]
    gathered = lax.all_gather(top.astype(jnp.bfloat16), "dp", axis=1, tiled=True).astype(top.dtype)
    mirror = lax.dynamic_slice_in_dim(gathered, part_idx * cols_loc, cols_loc, 0).T
    paired = jnp.where(tile == 0, 0.5 * (top + mirror), top)
    new_coef = jnp.concatenate([paired, shrunk[band:]], axis=0)
    logsum_local = jnp.sum(jnp.where(on_diag, jnp.log(safe), 0.0))
    absolute_local = jnp.sum(jnp.where(on_diag, 0.0, jnp.abs(coef)))
    quad_total, logsum, absolute = lax.psum(
        (quad_term, logsum_local, absolute_local), ("dp", "row", "col")
    )
    objective = quad_total / (2.0 * total) - logsum + PENALTY * absolute
    return (new_coef, objective)


def solution(mesh):
    return jax.shard_map(
        per_device,
        mesh=mesh,
        in_specs=(P("dp", ("row", "col")), P(("row", "col"), "dp")),
        out_specs=(P(("row", "col"), "dp"), P()),
        check_vma=False,
    )
```

profile of v0, /device:TPU:32, one launch (start us, length us, event | category | flops | bytes accessed | tf_op | source)
XLA Modules:
  0.0 1157.2 jit_solution(502436083019596381)
XLA Ops:
  7.2 0.0 all-gather.2.cloned.1.call-start
  7.2 1.6 convert_element_type.26
  8.8 0.0 all-gather.2.cloned.1.call-update
  8.9 0.0 all-reduce.3.cloned.1.call-start
  8.9 2.2 convert_reduce_fusion
  11.1 30.7 %psum.42 = f32[768]{0:T(1024)S(1)} all-reduce(f32[768]{0:T(1024)S(1)} %convert_reduce_fusion), channel_id=1, replica_groups=mesh['dp'=32,'row'=8,'col'=2] {'row','col'}, use_global_device_ids=true, to_apply=%region_1.0 | all-reduce | flops 768 | bytes 6144 | tf_op jit(solution)/shard_map/psum | solution.py:22
  41.8 1.4 fusion.9
  43.2 81.2 %psum.43 = f32[1024]{0:T(1024)S(1)} all-reduce(f32[1024]{0:T(1024)S(1)} %fusion.9), channel_id=1, replica_groups=mesh['dp'=32,'row'=8,'col'=2] {'dp'}, use_global_device_ids=true, to_apply=%region_3.0 | all-reduce | flops 1024 | bytes 8192 | tf_op jit(solution)/shard_map/psum | solution.py:24
  124.4 34.4 %all-gather.2.cloned.1.call-done = bf16[1024,512]{0,1:T(8,128)(2,1)} async-done(((bf16[1024,16]{0,1:T(8,128)(2,1)}), bf16[1024,512]{0,1:T(8,128)(2,1)}) %all-gather.2.cloned.1.call-update) | async-done | bytes 1048592 | tf_op jit(solution)/shard_map/all_gather | solution.py:29
  158.8 4.0 fusion.1
  162.8 0.0 all-reduce.3.cloned.1.call-update
  162.8 0.0 copy-start.1
  162.8 0.0 reduce-scatter.2.cloned.1.call-start
  162.9 137.6 %all-reduce.3.cloned.1.call-done = f32[768,512]{1,0:T(8,128)} async-done(((f32[768,512]{1,0:T(8,128)}), f32[768,512]{1,0:T(8,128)}) %all-reduce.3.cloned.1.call-update) | async-done | bytes 1572880 | tf_op jit(solution)/shard_map/psum | solution.py:32
  300.5 4.5 convolution_convert_fusion
  305.0 0.0 reduce-scatter.2.cloned.1.call-update
  305.0 2.4 multiply_reduce_fusion
  308.1 659.2 %reduce-scatter.2.cloned.1.call-done = bf16[16,1024]{1,0:T(8,128)(2,1)} async-done(((bf16[512,1024]{1,0:T(8,128)(2,1)}), bf16[16,1024]{1,0:T(8,128)(2,1)}) %reduce-scatter.2.cloned.1.call-update) | async-done | bytes 32784 | tf_op jit(solution)/shard_map/reduce_scatter | solution.py:35
  967.4 1.5 fusion.6
  968.8 74.5 %all_gather.7 = bf16[512,512]{0,1:T(8,128)(2,1)S(1)} all-gather(bf16[512,16]{0,1:T(8,128)(2,1)S(1)} %slice.12), channel_id=1, replica_groups=mesh['dp'=32,'row'=8,'col'=2] {'dp'}, dimensions={1}, use_global_device_ids=true | all-gather | bytes 540672 | tf_op jit(solution)/shard_map/all_gather | solution.py:54
  1043.4 0.1 constant_dynamic-slice_fusion
  1043.5 0.1 copy.6
  1043.6 103.3 %all-reduce = (f32[]{:T(128)}, f32[]{:T(128)}, f32[]{:T(128)}) all-reduce(f32[]{:T(128)S(6)} %div.43, f32[]{:T(128)} %get-tuple-element.3, f32[]{:T(128)} %get-tuple-element.2), channel_id=1, replica_groups=mesh['dp'=32,'row'=8,'col'=2] {'dp','row','col'}, use_global_device_ids=true, to_apply=%region_7.8 | all-reduce | flops 3 | bytes 24 | tf_op jit(solution)/shard_map/psum | solution.py:60
  1148.9 0.6 pad_maximum_fusion
  (9 shorter events, 0.0 us)
Async XLA Ops:
  7.2 34.7 %copy-start = (s32[768,1024]{1,0:T(8,128)S(1)}, s32[768,1024]{1,0:T(8,128)}, u32[]{:S(2)}) copy-start(s32[768,1024]{1,0:T(8,128)} %param.2) | copy-start | bytes 9437188
  7.2 151.6 %all-gather.2.cloned.1.call-start = ((), (), s32[]{:S(2)}) async-start(), calls=%async_computation.1 | async-start | bytes 1081344 | tf_op jit(solution)/shard_map/all_gather | solution.py:29
  8.9 291.6 %all-reduce.3.cloned.1.call-start = ((), (), s32[]{:S(2)}) async-start(), calls=%async_computation.2 | async-start | bytes 3145728 | tf_op jit(solution)/shard_map/psum | solution.py:32
  162.8 804.5 %copy-start.1 = (f32[1024,16]{0,1:T(8,128)S(1)}, f32[1024,16]{0,1:T(8,128)}, u32[]{:S(2)}) copy-start(f32[1024,16]{0,1:T(8,128)} %param.3) | copy-start | bytes 196612
  162.8 804.5 %reduce-scatter.2.cloned.1.call-start = ((), (), s32[]{:S(2)}) async-start(), calls=%async_computation.3 | async-start | bytes 1081344 | tf_op jit(solution)/shard_map/reduce_scatter | solution.py:35
Sparse Core Ops, SparseCore 0:
  11.7 147.0 all-gather.1
  162.9 137.5 all-reduce.2
  305.5 661.8 reduce-scatter.1
where the time goes:
time: 1160 us
  waiting for transfers between devices  831 us (72%)
  blocking collectives  290 us (25%)
  between operations  17.6 us (2%)
    reduce_scatter x1, waiting for transfers between devices, per_device(): lax.psum_scatter(lax.dot_general(projection_low, centered, (((0,), (0,)),...  659 us
    psum x1, waiting for transfers between devices, per_device(): projection = lax.psum(partial_proj, ('row', 'col'))  138 us
    psum x1, blocking collectives, per_device(): lax.psum((quad_term, logsum_local, absolute_local), ('dp', 'row', 'col'))  103 us
    psum x1, blocking collectives, per_device(): means = lax.psum(jnp.sum(expression, axis=0), 'dp') / total  81.2 us
    all_gather x1, blocking collectives, per_device(): lax.all_gather(top.astype(jnp.bfloat16), 'dp', axis=1, tiled=True)  74.5 us
    all_gather x1, waiting for transfers between devices, per_device(): lax.all_gather(coef_low, 'dp', axis=1, tiled=True)  34.4 us
    psum x1, blocking collectives, per_device(): library = lax.psum(jnp.sum(counts_f, axis=1), ('row', 'col'))  30.7 us
  transfers between devices with their start and end apart: 3, of which 3 were waited for; matrix products, arithmetic and copies ran while one was open for 1% of the time, Pallas kernels for 0%

commit v1 on v0

v1 whole, which is shorter than its diff:
```python
import jax
import jax.numpy as jnp
from jax import lax
from jax.sharding import Mesh, PartitionSpec as P

STEP = 0.5
PENALTY = 0.05
SCALE = 10000.0

FAR = "zh"
NEAR = ("zl", "xh")
TILE = ("y", "core", "xl")
AXES = (FAR,) + NEAR + TILE
SIZES = (8, 2, 2, 4, 2, 2)
N_FAR, N_NEAR, N_TILE = 8, 4, 16
EXTRA = 8


def spread(block, axes, n):
    return lax.all_to_all(jnp.broadcast_to(block[None], (n,) + block.shape), axes, 0, 0)


def split3(v):
    hi = lax.reduce_precision(v, 8, 7)
    rest = v - hi
    mid = lax.reduce_precision(rest, 8, 7)
    return [a.astype(jnp.bfloat16) for a in (hi, mid, rest - mid)]


def join3(rows):
    rows = rows.astype(jnp.float32)
    return (rows[:, 2] + rows[:, 1]) + rows[:, 0]


def outer_sum(left, right):
    return sum(left[i][:, None] * right[i][None, :] for i in range(left.shape[0]))


def extras(means, w, scalars):
    vec = jnp.concatenate([means, w])
    sc = jnp.pad(jnp.stack(scalars), (0, vec.shape[0] - len(scalars)))
    rows = split3(vec) + split3(sc)
    rows += [jnp.zeros_like(rows[0])] * (EXTRA - len(rows))
    return jnp.stack(rows)


def read_extras(rows, genes):
    vec = join3(rows[:, 0:3])
    sc = join3(rows[:, 3:6, :128])
    return vec[:, :genes], vec[:, genes:], [sc[:, i] for i in range(3)]


def per_device(counts, coef):
    cells, genes = counts.shape
    cols = coef.shape[1]
    n_dp = N_FAR * N_NEAR
    band = cols * n_dp
    total = float(cells * n_dp)
    tile = lax.axis_index(TILE)
    near = lax.axis_index(NEAR)
    far = lax.axis_index(FAR)
    part = far * N_NEAR + near
    f32, bf16 = jnp.float32, jnp.bfloat16

    coef_t = coef.T
    w_far = spread(coef_t.astype(bf16), FAR, N_FAR).reshape(N_FAR * cols, genes)
    weights = spread(w_far, NEAR, N_NEAR).reshape(band, genes)

    rows_id = lax.broadcasted_iota(jnp.int32, (cols, genes), 1) + tile * genes
    cols_id = lax.broadcasted_iota(jnp.int32, (cols, genes), 0) + part * cols
    on_diag = rows_id == cols_id
    safe = jnp.where(on_diag, coef_t, 1.0)
    logsum = jnp.sum(jnp.where(on_diag, jnp.log(safe), 0.0))
    absolute = jnp.sum(jnp.where(on_diag, 0.0, jnp.abs(coef_t)))

    lib_rows = cells // 128
    lib = jnp.sum(counts, axis=1).astype(f32).reshape(lib_rows, 128)
    sums = jnp.pad(jnp.stack([logsum, absolute])[None], ((0, 7 - lib_rows % 8), (0, 126)))
    head = jnp.sum(spread(jnp.concatenate([lib, sums]), TILE, N_TILE), axis=0)
    library = head[:lib_rows].reshape(cells)
    logsum, absolute = head[lib_rows, 0], head[lib_rows, 1]

    scale = SCALE / (library + 1.0)
    expr = jnp.log(1.0 + counts.astype(f32) * scale[:, None]).astype(bf16)
    expr = lax.optimization_barrier(expr)
    sums_e = jnp.sum(expr.astype(f32), axis=0)

    partial = lax.dot_general(weights, expr, (((1,), (1,)), ((), ())), preferred_element_type=f32)
    got = lax.all_to_all(partial.astype(bf16).reshape(N_TILE, band // N_TILE, cells), TILE, 0, 0)
    mine = jnp.sum(got.astype(f32), axis=0).astype(bf16)
    proj = spread(mine, TILE, N_TILE).reshape(band, cells)

    proj_f = proj.astype(f32)
    w = jnp.sum(proj_f, axis=1) / cells
    quad = jnp.sum(proj_f * proj_f) - cells * jnp.sum(w * w)
    means = sums_e / cells
    covar = lax.dot_general(proj, expr, (((1,), (0,)), ((), ())), preferred_element_type=f32)
    covar = (covar - w[:, None] * sums_e[None, :]).astype(bf16)
    natural = covar[:, :band].reshape(N_NEAR, N_FAR, cols, band).transpose(1, 0, 2, 3)
    mirror = natural.reshape(band, band).T
    mirror = mirror.reshape(N_FAR, N_NEAR, cols, band).transpose(1, 0, 2, 3)
    main = jnp.concatenate(
        [
            covar.reshape(N_NEAR, N_FAR * cols, genes),
            mirror.reshape(N_NEAR, N_FAR * cols, band),
        ],
        axis=2,
    )
    w_nat = w.reshape(N_NEAR, N_FAR, cols).transpose(1, 0, 2).reshape(band)
    more = extras(means, w_nat, [quad, logsum, absolute])
    more = jnp.broadcast_to(more[None], (N_NEAR,) + more.shape)
    got = lax.all_to_all(jnp.concatenate([main, more], axis=1), NEAR, 0, 0)

    def of_near(v):
        v = v.reshape(-1, N_FAR, N_NEAR, cols)
        return lax.dynamic_index_in_dim(v, near, 2, False).reshape(-1, N_FAR * cols)

    def merge(got, weight, pick):
        n, rows = got.shape[0], got.shape[1] - EXTRA
        means, w, (quad, logsum, absolute) = read_extras(got[:, rows:], genes)
        means_all = jnp.sum(means, axis=0) / n
        w_all = jnp.sum(w, axis=0) / n
        dm, dw = means - means_all, w - w_all
        total_a = jnp.sum(got[:, :rows, :genes].astype(f32), axis=0)
        total_b = jnp.sum(got[:, :rows, genes:].astype(f32), axis=0)
        total_a += outer_sum(pick(dw) * weight, dm)
        total_b += outer_sum(pick(dm[:, :band]) * weight, dw)
        quad = jnp.sum(quad) + weight * jnp.sum(dw * dw)
        return total_a, total_b, means_all, w_all, quad, jnp.sum(logsum), jnp.sum(absolute)

    total_a, total_b, means, w, quad, logsum, absolute = merge(got, float(cells), of_near)
    main = jnp.concatenate([total_a, total_b], axis=1).astype(bf16)
    main = main.reshape(N_FAR, cols, genes + band)
    more = extras(means, w, [quad, logsum, absolute])
    more = jnp.broadcast_to(more[None], (N_FAR,) + more.shape)
    got = lax.all_to_all(jnp.concatenate([main, more], axis=1), FAR, 0, 0)

    def of_part(v):
        return lax.dynamic_slice_in_dim(v, part * cols, cols, 1)

    total_a, total_b, _, _, quad, logsum, absolute = merge(got, float(cells * N_NEAR), of_part)
    inverse = jnp.where(on_diag, 1.0 / safe, 0.0)
    stepped = coef_t - STEP * (total_a / total - inverse)
    limit = STEP * PENALTY
    shrunk = jnp.where(on_diag, stepped, stepped - jnp.clip(stepped, -limit, limit))

    coef_m = lax.dynamic_slice_in_dim(weights, part * cols, cols, 1)
    coef_m = coef_m.reshape(N_NEAR, N_FAR, cols, cols).transpose(1, 0, 2, 3).reshape(band, cols)
    stepped_m = coef_m.T.astype(f32) - STEP * (total_b / total)
    shrunk_m = stepped_m - jnp.clip(stepped_m, -limit, limit)
    top = shrunk[:, :band]
    use = jnp.logical_and(tile == 0, jnp.logical_not(on_diag[:, :band]))
    paired = jnp.where(use, 0.5 * (top + shrunk_m), top)
    new_coef = jnp.concatenate([paired, shrunk[:, band:]], axis=1).T
    objective = quad / (2.0 * total) - logsum + PENALTY * absolute
    return (new_coef, objective)


def solution(mesh):
    mesh = Mesh(mesh.devices.reshape(SIZES), AXES)
    return jax.shard_map(
        per_device,
        mesh=mesh,
        in_specs=(P((FAR,) + NEAR, TILE), P(TILE, (FAR,) + NEAR)),
        out_specs=(P(TILE, (FAR,) + NEAR), P()),
        check_vma=False,
    )
```

time: 1160 us -> 197 us (0.17)
  the two profiles are of different devices: /device:TPU:32 before, /device:TPU:6 now
where the time goes in v1:
time: 197 us; the launch traced here: 196 us
  waiting for transfers between devices  99.6 us (51%)
  starting transfers between devices  39.9 us (20%)
  other arithmetic  22.6 us (11%)
  blocking collectives  16.1 us (8%)
  local copies, waits for them, and re-layouts  8.32 us (4%)
  between operations  7.36 us (4%)
  matrix products  2.01 us (1%)
    all_to_all x4, waiting for transfers between devices, spread(): lax.all_to_all(jnp.broadcast_to(block[None], (n,) + block.shape), axes, 0...  45.1 us
    all_to_all x1, waiting for transfers between devices, per_device(): got = lax.all_to_all(jnp.concatenate([main, more], axis=1), FAR, 0, 0)  33.9 us
    all_to_all x4, starting transfers between devices, spread(): lax.all_to_all(jnp.broadcast_to(block[None], (n,) + block.shape), axes, 0...  30.7 us
    all_to_all x1, waiting for transfers between devices, per_device(): got = lax.all_to_all(jnp.concatenate([main, more], axis=1), NEAR, 0, 0)  20.6 us
    all_to_all x1, blocking collectives, per_device(): lax.all_to_all(partial.astype(bf16).reshape(N_TILE, band // N_TILE, cells...  16.1 us
    convert_element_type x7, other arithmetic, split3(): return [a.astype(jnp.bfloat16) for a in (hi, mid, rest - mid)]  6.8 us
    all_to_all x1, starting transfers between devices, per_device(): got = lax.all_to_all(jnp.concatenate([main, more], axis=1), NEAR, 0, 0)  5.64 us
  transfers between devices with their start and end apart: 6, of which 6 were waited for; matrix products, arithmetic and copies ran while one was open for 4% of the time, Pallas kernels for 0%

profile of v1, /device:TPU:6, one launch (start us, length us, event | category | flops | bytes accessed | tf_op | source)
XLA Modules:
  0.0 196.0 jit_solution(12829530850201098379)
XLA Ops:
  2.2 15.1 %all-to-all-start.1 = ((bf16[8,16,1024]{2,1,0:T(8,128)(2,1)}), bf16[8,16,1024]{2,1,0:T(8,128)(2,1)S(1)}, u32[]{:S(2)}, u32[]{:S(2)}) async-start(bf16[8,16,1024]{2,1,0:T(8,128)(2,1)} %broadcast_in_dim.30), calls=%async_computation.1 | async-start | bytes 524288 | tf_op jit(solution)/shard_map/all_to_all | solution.py:20
  17.3 2.1 %reduce_sum.232 = s32[768]{0:T(1024)S(1)} reduce(s32[768,1024]{1,0:T(8,128)} %param.2, s32[]{:T(128)} %constant.33.clone.1), dimensions={1}, to_apply=%region_0.1 | reduce | flops 785664 | bytes 3148804 | tf_op jit(solution)/shard_map/reduce_sum | solution.py:77
  20.2 1.4 maximum_bitcast_fusion.1
  21.6 17.1 %all-to-all-done.1 = bf16[8,16,1024]{2,1,0:T(8,128)(2,1)S(1)} async-done(((bf16[8,16,1024]{2,1,0:T(8,128)(2,1)}), bf16[8,16,1024]{2,1,0:T(8,128)(2,1)S(1)}, u32[]{:S(2)}, u32[]{:S(2)}) %all-to-all-start.1) | async-done | bytes 262176 | tf_op jit(solution)/shard_map/all_to_all | solution.py:20
  39.3 5.9 %all-to-all-start = ((f32[16,8,128]{2,1,0:T(8,128)}), f32[16,8,128]{2,1,0:T(8,128)S(1)}, u32[]{:S(2)}, u32[]{:S(2)}) async-start(f32[16,8,128]{2,1,0:T(8,128)} %broadcast_in_dim.29), calls=%async_computation | async-start | bytes 131072 | tf_op jit(solution)/shard_map/all_to_all | solution.py:20
  45.4 4.8 %all-to-all-done = f32[16,8,128]{2,1,0:T(8,128)S(1)} async-done(((f32[16,8,128]{2,1,0:T(8,128)}), f32[16,8,128]{2,1,0:T(8,128)S(1)}, u32[]{:S(2)}, u32[]{:S(2)}) %all-to-all-start) | async-done | bytes 65568 | tf_op jit(solution)/shard_map/all_to_all | solution.py:20
  50.3 1.1 broadcast_in_dim.32
  51.4 5.6 %all-to-all-start.2 = ((bf16[4,128,1024]{1,2,0:T(8,128)(2,1)}), bf16[4,128,1024]{1,2,0:T(8,128)(2,1)}, u32[]{:S(2)}, u32[]{:S(2)}) async-start(bf16[4,128,1024]{1,2,0:T(8,128)(2,1)} %broadcast_in_dim.32), calls=%async_computation.2 | async-start | bytes 2097152 | tf_op jit(solution)/shard_map/all_to_all | solution.py:20
  57.0 1.8 log_convert_fusion
  58.8 11.9 %all-to-all-done.2 = bf16[4,128,1024]{1,2,0:T(8,128)(2,1)} async-done(((bf16[4,128,1024]{1,2,0:T(8,128)(2,1)}), bf16[4,128,1024]{1,2,0:T(8,128)(2,1)}, u32[]{:S(2)}, u32[]{:S(2)}) %all-to-all-start.2) | async-done | bytes 1048608 | tf_op jit(solution)/shard_map/all_to_all | solution.py:20
  70.7 1.5 copy.47
  73.3 16.1 %all_to_all.35 = bf16[16,32,768]{2,1,0:T(8,128)(2,1)S(1)} all-to-all(bf16[16,32,768]{2,1,0:T(8,128)(2,1)S(1)} %bitcast.147), channel_id=1, replica_groups=mesh['zh'=8,'zl'=2,'xh'=2,'y'=4,'core'=2,'xl'=2] {'y','core','xl'}, dimensions={0} | all-to-all | bytes 1572864 | tf_op jit(solution)/shard_map/all_to_all | solution.py:89
  90.5 4.1 %all-to-all-start.4 = ((bf16[16,32,768]{2,1,0:T(8,128)(2,1)}), bf16[16,32,768]{2,1,0:T(8,128)(2,1)S(1)}, u32[]{:S(2)}, u32[]{:S(2)}) async-start(bf16[16,32,768]{2,1,0:T(8,128)(2,1)} %broadcast_in_dim.33), calls=%async_computation.4 | async-start | bytes 1572864 | tf_op jit(solution)/shard_map/all_to_all | solution.py:20
  95.5 11.2 %all-to-all-done.4 = bf16[16,32,768]{2,1,0:T(8,128)(2,1)S(1)} async-done(((bf16[16,32,768]{2,1,0:T(8,128)(2,1)}), bf16[16,32,768]{2,1,0:T(8,128)(2,1)S(1)}, u32[]{:S(2)}, u32[]{:S(2)}) %all-to-all-start.4) | async-done | bytes 786464 | tf_op jit(solution)/shard_map/all_to_all | solution.py:20
  109.6 1.3 fusion.10
  110.8 1.3 reduce-precision_convert_fusion.2
  113.8 1.3 pad_maximum_fusion
  115.2 5.6 %all-to-all-start.5 = ((bf16[4,136,1536]{2,1,0:T(8,128)(2,1)}), bf16[4,136,1536]{2,1,0:T(8,128)(2,1)S(1)}, u32[]{:S(2)}, u32[]{:S(2)}) async-start(bf16[4,136,1536]{2,1,0:T(8,128)(2,1)} %pad_maximum_fusion), calls=%async_computation.5 | async-start | bytes 3342336 | tf_op jit(solution)/shard_map/all_to_all | solution.py:112
  120.8 20.6 %all-to-all-done.5 = bf16[4,136,1536]{2,1,0:T(8,128)(2,1)S(1)} async-done(((bf16[4,136,1536]{2,1,0:T(8,128)(2,1)}), bf16[4,136,1536]{2,1,0:T(8,128)(2,1)S(1)}, u32[]{:S(2)}, u32[]{:S(2)}) %all-to-all-start.5) | async-done | bytes 1671200 | tf_op jit(solution)/shard_map/all_to_all | solution.py:112
  144.2 1.4 reduce-precision_convert_fusion.1
  145.6 1.4 fusion.11
  147.0 1.4 reduce-precision_convert_fusion
  150.4 3.5 %all-to-all-start.6 = ((bf16[8,24,1536]{2,1,0:T(8,128)(2,1)}), bf16[8,24,1536]{2,1,0:T(8,128)(2,1)S(1)}, u32[]{:S(2)}, u32[]{:S(2)}) async-start(bf16[8,24,1536]{2,1,0:T(8,128)(2,1)} %pad_maximum_fusion.1), calls=%async_computation.6 | async-start | bytes 1179648 | tf_op jit(solution)/shard_map/all_to_all | solution.py:136
  155.6 33.9 %all-to-all-done.6 = bf16[8,24,1536]{2,1,0:T(8,128)(2,1)S(1)} async-done(((bf16[8,24,1536]{2,1,0:T(8,128)(2,1)}), bf16[8,24,1536]{2,1,0:T(8,128)(2,1)S(1)}, u32[]{:S(2)}, u32[]{:S(2)}) %all-to-all-start.6) | async-done | bytes 589856 | tf_op jit(solution)/shard_map/all_to_all | solution.py:136
  (106 shorter events, 17.0 us)
Async XLA Ops:
  2.2 36.5 %all-to-all-start.1 = ((bf16[8,16,1024]{2,1,0:T(8,128)(2,1)}), bf16[8,16,1024]{2,1,0:T(8,128)(2,1)S(1)}, u32[]{:S(2)}, u32[]{:S(2)}) async-start(bf16[8,16,1024]{2,1,0:T(8,128)(2,1)} %broadcast_in_dim.30), calls=%async_computation.1 | async-start | bytes 524288 | tf_op jit(solution)/shard_map/all_to_all | solution.py:20
  17.3 2.2 %copy-start.3 = (f32[1024,16]{0,1:T(8,128)S(1)}, f32[1024,16]{0,1:T(8,128)}, u32[]{:S(2)}) copy-start(f32[1024,16]{0,1:T(8,128)} %param.3) | copy-start | bytes 196612
  39.3 11.0 %all-to-all-start = ((f32[16,8,128]{2,1,0:T(8,128)}), f32[16,8,128]{2,1,0:T(8,128)S(1)}, u32[]{:S(2)}, u32[]{:S(2)}) async-start(f32[16,8,128]{2,1,0:T(8,128)} %broadcast_in_dim.29), calls=%async_computation | async-start | bytes 131072 | tf_op jit(solution)/shard_map/all_to_all | solution.py:20
  45.4 11.6 %copy-start = (s32[768,1024]{1,0:T(8,128)S(1)}, s32[768,1024]{1,0:T(8,128)}, u32[]{:S(2)}) copy-start(s32[768,1024]{1,0:T(8,128)} %param.2) | copy-start | bytes 9437188
  51.4 19.4 %all-to-all-start.2 = ((bf16[4,128,1024]{1,2,0:T(8,128)(2,1)}), bf16[4,128,1024]{1,2,0:T(8,128)(2,1)}, u32[]{:S(2)}, u32[]{:S(2)}) async-start(bf16[4,128,1024]{1,2,0:T(8,128)(2,1)} %broadcast_in_dim.32), calls=%async_computation.2 | async-start | bytes 2097152 | tf_op jit(solution)/shard_map/all_to_all | solution.py:20
  58.8 13.4 %copy-start.1 = (bf16[768,1024]{1,0:T(8,128)(2,1)S(1)}, bf16[768,1024]{1,0:T(8,128)(2,1)}, u32[]{:S(2)}) copy-start(bf16[768,1024]{1,0:T(8,128)(2,1)} %log_convert_fusion) | copy-start | bytes 4718596
  72.2 1.1 copy-start.2
  90.5 16.2 %all-to-all-start.4 = ((bf16[16,32,768]{2,1,0:T(8,128)(2,1)}), bf16[16,32,768]{2,1,0:T(8,128)(2,1)S(1)}, u32[]{:S(2)}, u32[]{:S(2)}) async-start(bf16[16,32,768]{2,1,0:T(8,128)(2,1)} %broadcast_in_dim.33), calls=%async_computation.4 | async-start | bytes 1572864 | tf_op jit(solution)/shard_map/all_to_all | solution.py:20
  115.2 26.3 %all-to-all-start.5 = ((bf16[4,136,1536]{2,1,0:T(8,128)(2,1)}), bf16[4,136,1536]{2,1,0:T(8,128)(2,1)S(1)}, u32[]{:S(2)}, u32[]{:S(2)}) async-start(bf16[4,136,1536]{2,1,0:T(8,128)(2,1)} %pad_maximum_fusion), calls=%async_computation.5 | async-start | bytes 3342336 | tf_op jit(solution)/shard_map/all_to_all | solution.py:112
  150.4 39.1 %all-to-all-start.6 = ((bf16[8,24,1536]{2,1,0:T(8,128)(2,1)}), bf16[8,24,1536]{2,1,0:T(8,128)(2,1)S(1)}, u32[]{:S(2)}, u32[]{:S(2)}) async-start(bf16[8,24,1536]{2,1,0:T(8,128)(2,1)} %pad_maximum_fusion.1), calls=%async_computation.6 | async-start | bytes 1179648 | tf_op jit(solution)/shard_map/all_to_all | solution.py:136

commit v2 on v1

--- a/solution.py
+++ b/solution.py
@@ -64,7 +64,6 @@
 
     coef_t = coef.T
     w_far = spread(coef_t.astype(bf16), FAR, N_FAR).reshape(N_FAR * cols, genes)
-    weights = spread(w_far, NEAR, N_NEAR).reshape(band, genes)
 
     rows_id = lax.broadcasted_iota(jnp.int32, (cols, genes), 1) + tile * genes
     cols_id = lax.broadcasted_iota(jnp.int32, (cols, genes), 0) + part * cols
@@ -76,7 +75,10 @@
     lib_rows = cells // 128
     lib = jnp.sum(counts, axis=1).astype(f32).reshape(lib_rows, 128)
     sums = jnp.pad(jnp.stack([logsum, absolute])[None], ((0, 7 - lib_rows % 8), (0, 126)))
-    head = jnp.sum(spread(jnp.concatenate([lib, sums]), TILE, N_TILE), axis=0)
+    head = lax.psum(lax.psum(jnp.concatenate([lib, sums]), "core"), "xl")
+    w_far, head = lax.optimization_barrier((w_far, head))
+    weights = spread(w_far, NEAR, N_NEAR).reshape(band, genes)
+    head = lax.psum(head, "y")
     library = head[:lib_rows].reshape(cells)
     logsum, absolute = head[lib_rows, 0], head[lib_rows, 1]
 

time: 197 us -> 185 us (0.939)
  the two profiles are of different devices: /device:TPU:6 before, /device:TPU:32 now
where the time goes in v2:
time: 185 us; the launch traced here: 184 us
  waiting for transfers between devices  74.2 us (40%)
  starting transfers between devices  35.4 us (19%)
  blocking collectives  34.2 us (18%)
  other arithmetic  22.6 us (12%)
  local copies, waits for them, and re-layouts  7.9 us (4%)
  between operations  7.34 us (4%)
  matrix products  2.01 us (1%)
    all_to_all x1, waiting for transfers between devices, per_device(): got = lax.all_to_all(jnp.concatenate([main, more], axis=1), FAR, 0, 0)  32.1 us
    all_to_all x3, starting transfers between devices, spread(): lax.all_to_all(jnp.broadcast_to(block[None], (n,) + block.shape), axes, 0...  24.2 us
    all_to_all x1, waiting for transfers between devices, per_device(): got = lax.all_to_all(jnp.concatenate([main, more], axis=1), NEAR, 0, 0)  21.8 us
    all_to_all x3, waiting for transfers between devices, spread(): lax.all_to_all(jnp.broadcast_to(block[None], (n,) + block.shape), axes, 0...  20.3 us
    all_to_all x1, blocking collectives, per_device(): lax.all_to_all(partial.astype(bf16).reshape(N_TILE, band // N_TILE, cells...  16.1 us
    psum x1, blocking collectives, per_device(): head = lax.psum(head, 'y')  10.7 us
    psum x2, blocking collectives, per_device(): head = lax.psum(lax.psum(jnp.concatenate([lib, sums]), 'core'), 'xl')  7.39 us
    convert_element_type x7, other arithmetic, split3(): return [a.astype(jnp.bfloat16) for a in (hi, mid, rest - mid)]  6.8 us
  transfers between devices with their start and end apart: 5, of which 4 were waited for; matrix products, arithmetic and copies ran while one was open for 5% of the time, Pallas kernels for 0%

profile of v2, /device:TPU:32, one launch (start us, length us, event | category | flops | bytes accessed | tf_op | source)
XLA Modules:
  0.0 183.7 jit_solution(17325738166243514653)
XLA Ops:
  2.2 14.2 %all-to-all-start = ((bf16[8,16,1024]{2,1,0:T(8,128)(2,1)}), bf16[8,16,1024]{2,1,0:T(8,128)(2,1)S(1)}, u32[]{:S(2)}, u32[]{:S(2)}) async-start(bf16[8,16,1024]{2,1,0:T(8,128)(2,1)} %broadcast_in_dim.22), calls=%async_computation | async-start | bytes 524288 | tf_op jit(solution)/shard_map/all_to_all | solution.py:20
  16.4 2.1 %reduce_sum.223 = s32[768]{0:T(1024)S(1)} reduce(s32[768,1024]{1,0:T(8,128)} %param.2, s32[]{:T(128)} %constant.33.clone.1), dimensions={1}, to_apply=%region_0.1 | reduce | flops 785664 | bytes 3148804 | tf_op jit(solution)/shard_map/reduce_sum | solution.py:76
  19.3 1.4 maximum_bitcast_fusion.1
  20.7 2.5 %psum.21 = f32[8,128]{1,0:T(8,128)S(1)} all-reduce(f32[8,128]{1,0:T(8,128)S(1)} %select_maximum_fusion.4), channel_id=1, replica_groups=mesh['zh'=8,'zl'=2,'xh'=2,'y'=4,'core'=2,'xl'=2] {'core'}, use_global_device_ids=true, to_apply=%region_3.4 | all-reduce | flops 1024 | bytes 8192 | tf_op jit(solution)/shard_map/psum | solution.py:78
  23.1 4.9 %psum.22 = f32[8,128]{1,0:T(8,128)S(1)} all-reduce(f32[8,128]{1,0:T(8,128)S(1)} %psum.21), channel_id=1, replica_groups=mesh['zh'=8,'zl'=2,'xh'=2,'y'=4,'core'=2,'xl'=2] {'xl'}, use_global_device_ids=true, to_apply=%region_4.5 | all-reduce | flops 1024 | bytes 8192 | tf_op jit(solution)/shard_map/psum | solution.py:78
  28.0 8.7 %all-to-all-done = bf16[8,16,1024]{2,1,0:T(8,128)(2,1)S(1)} async-done(((bf16[8,16,1024]{2,1,0:T(8,128)(2,1)}), bf16[8,16,1024]{2,1,0:T(8,128)(2,1)S(1)}, u32[]{:S(2)}, u32[]{:S(2)}) %all-to-all-start) | async-done | bytes 262176 | tf_op jit(solution)/shard_map/all_to_all | solution.py:20
  37.0 1.1 broadcast_in_dim.26
  38.1 6.4 %all-to-all-start.1 = ((bf16[4,128,1024]{1,2,0:T(8,128)(2,1)}), bf16[4,128,1024]{1,2,0:T(8,128)(2,1)}, u32[]{:S(2)}, u32[]{:S(2)}) async-start(bf16[4,128,1024]{1,2,0:T(8,128)(2,1)} %broadcast_in_dim.26), calls=%async_computation.1 | async-start | bytes 2097152 | tf_op jit(solution)/shard_map/all_to_all | solution.py:20
  44.5 10.7 %psum.23 = f32[8,128]{1,0:T(8,128)S(1)} all-reduce(f32[8,128]{1,0:T(8,128)S(1)} %psum.22), channel_id=1, replica_groups=mesh['zh'=8,'zl'=2,'xh'=2,'y'=4,'core'=2,'xl'=2] {'y'}, use_global_device_ids=true, to_apply=%region_5.6 | all-reduce | flops 1024 | bytes 8192 | tf_op jit(solution)/shard_map/psum | solution.py:81
  55.2 1.8 log_convert_fusion
  57.0 1.6 copy.47
  59.8 16.1 %all_to_all.30 = bf16[16,32,768]{2,1,0:T(8,128)(2,1)S(1)} all-to-all(bf16[16,32,768]{2,1,0:T(8,128)(2,1)S(1)} %bitcast.145), channel_id=1, replica_groups=mesh['zh'=8,'zl'=2,'xh'=2,'y'=4,'core'=2,'xl'=2] {'y','core','xl'}, dimensions={0} | all-to-all | bytes 1572864 | tf_op jit(solution)/shard_map/all_to_all | solution.py:91
  76.9 3.6 %all-to-all-start.3 = ((bf16[16,32,768]{2,1,0:T(8,128)(2,1)}), bf16[16,32,768]{2,1,0:T(8,128)(2,1)S(1)}, u32[]{:S(2)}, u32[]{:S(2)}) async-start(bf16[16,32,768]{2,1,0:T(8,128)(2,1)} %broadcast_in_dim.27), calls=%async_computation.3 | async-start | bytes 1572864 | tf_op jit(solution)/shard_map/all_to_all | solution.py:20
  81.4 11.5 %all-to-all-done.3 = bf16[16,32,768]{2,1,0:T(8,128)(2,1)S(1)} async-done(((bf16[16,32,768]{2,1,0:T(8,128)(2,1)}), bf16[16,32,768]{2,1,0:T(8,128)(2,1)S(1)}, u32[]{:S(2)}, u32[]{:S(2)}) %all-to-all-start.3) | async-done | bytes 786464 | tf_op jit(solution)/shard_map/all_to_all | solution.py:20
  95.9 1.3 fusion.10
  97.1 1.3 reduce-precision_convert_fusion.2
  100.2 1.3 pad_maximum_fusion
  101.5 6.1 %all-to-all-start.4 = ((bf16[4,136,1536]{2,1,0:T(8,128)(2,1)}), bf16[4,136,1536]{2,1,0:T(8,128)(2,1)S(1)}, u32[]{:S(2)}, u32[]{:S(2)}) async-start(bf16[4,136,1536]{2,1,0:T(8,128)(2,1)} %pad_maximum_fusion), calls=%async_computation.4 | async-start | bytes 3342336 | tf_op jit(solution)/shard_map/all_to_all | solution.py:114
  107.6 21.8 %all-to-all-done.4 = bf16[4,136,1536]{2,1,0:T(8,128)(2,1)S(1)} async-done(((bf16[4,136,1536]{2,1,0:T(8,128)(2,1)}), bf16[4,136,1536]{2,1,0:T(8,128)(2,1)S(1)}, u32[]{:S(2)}, u32[]{:S(2)}) %all-to-all-start.4) | async-done | bytes 1671200 | tf_op jit(solution)/shard_map/all_to_all | solution.py:114
  132.1 1.4 reduce-precision_convert_fusion.1
  133.5 1.4 fusion.11
  134.9 1.4 reduce-precision_convert_fusion
  138.4 5.1 %all-to-all-start.5 = ((bf16[8,24,1536]{2,1,0:T(8,128)(2,1)}), bf16[8,24,1536]{2,1,0:T(8,128)(2,1)S(1)}, u32[]{:S(2)}, u32[]{:S(2)}) async-start(bf16[8,24,1536]{2,1,0:T(8,128)(2,1)} %pad_maximum_fusion.1), calls=%async_computation.5 | async-start | bytes 1179648 | tf_op jit(solution)/shard_map/all_to_all | solution.py:138
  145.1 32.1 %all-to-all-done.5 = bf16[8,24,1536]{2,1,0:T(8,128)(2,1)S(1)} async-done(((bf16[8,24,1536]{2,1,0:T(8,128)(2,1)}), bf16[8,24,1536]{2,1,0:T(8,128)(2,1)S(1)}, u32[]{:S(2)}, u32[]{:S(2)}) %all-to-all-start.5) | async-done | bytes 589856 | tf_op jit(solution)/shard_map/all_to_all | solution.py:138
  (105 shorter events, 16.4 us)
Async XLA Ops:
  2.2 34.6 %all-to-all-start = ((bf16[8,16,1024]{2,1,0:T(8,128)(2,1)}), bf16[8,16,1024]{2,1,0:T(8,128)(2,1)S(1)}, u32[]{:S(2)}, u32[]{:S(2)}) async-start(bf16[8,16,1024]{2,1,0:T(8,128)(2,1)} %broadcast_in_dim.22), calls=%async_computation | async-start | bytes 524288 | tf_op jit(solution)/shard_map/all_to_all | solution.py:20
  16.4 2.2 %copy-start.3 = (f32[1024,16]{0,1:T(8,128)S(1)}, f32[1024,16]{0,1:T(8,128)}, u32[]{:S(2)}) copy-start(f32[1024,16]{0,1:T(8,128)} %param.3) | copy-start | bytes 196612
  36.9 18.3 %copy-start = (s32[768,1024]{1,0:T(8,128)S(1)}, s32[768,1024]{1,0:T(8,128)}, u32[]{:S(2)}) copy-start(s32[768,1024]{1,0:T(8,128)} %param.2) | copy-start | bytes 9437188
  38.1 18.9 %all-to-all-start.1 = ((bf16[4,128,1024]{1,2,0:T(8,128)(2,1)}), bf16[4,128,1024]{1,2,0:T(8,128)(2,1)}, u32[]{:S(2)}, u32[]{:S(2)}) async-start(bf16[4,128,1024]{1,2,0:T(8,128)(2,1)} %broadcast_in_dim.26), calls=%async_computation.1 | async-start | bytes 2097152 | tf_op jit(solution)/shard_map/all_to_all | solution.py:20
  57.0 1.7 copy-start.1
  58.6 1.1 copy-start.2
  76.9 16.0 %all-to-all-start.3 = ((bf16[16,32,768]{2,1,0:T(8,128)(2,1)}), bf16[16,32,768]{2,1,0:T(8,128)(2,1)S(1)}, u32[]{:S(2)}, u32[]{:S(2)}) async-start(bf16[16,32,768]{2,1,0:T(8,128)(2,1)} %broadcast_in_dim.27), calls=%async_computation.3 | async-start | bytes 1572864 | tf_op jit(solution)/shard_map/all_to_all | solution.py:20
  101.5 27.9 %all-to-all-start.4 = ((bf16[4,136,1536]{2,1,0:T(8,128)(2,1)}), bf16[4,136,1536]{2,1,0:T(8,128)(2,1)S(1)}, u32[]{:S(2)}, u32[]{:S(2)}) async-start(bf16[4,136,1536]{2,1,0:T(8,128)(2,1)} %pad_maximum_fusion), calls=%async_computation.4 | async-start | bytes 3342336 | tf_op jit(solution)/shard_map/all_to_all | solution.py:114
  138.4 38.9 %all-to-all-start.5 = ((bf16[8,24,1536]{2,1,0:T(8,128)(2,1)}), bf16[8,24,1536]{2,1,0:T(8,128)(2,1)S(1)}, u32[]{:S(2)}, u32[]{:S(2)}) async-start(bf16[8,24,1536]{2,1,0:T(8,128)(2,1)} %pad_maximum_fusion.1), calls=%async_computation.5 | async-start | bytes 1179648 | tf_op jit(solution)/shard_map/all_to_all | solution.py:138

commit v3 on v2

v3 whole, which is shorter than its diff:
```python
import functools

import jax
import jax.numpy as jnp
from jax import lax
from jax.experimental import pallas as pl
from jax.experimental.pallas import tpu as pltpu
from jax.sharding import Mesh, PartitionSpec as P

STEP = 0.5
PENALTY = 0.05
SCALE = 10000.0

FAR = "zh"
NEAR = ("zl", "xh")
TILE = ("y", "core", "xl")
AXES = (FAR,) + NEAR + TILE
SIZES = (8, 2, 2, 4, 2, 2)
N_FAR, N_NEAR, N_TILE = 8, 4, 16
EXTRA = 16


def spread(block, axes, n):
    return lax.all_to_all(jnp.broadcast_to(block[None], (n,) + block.shape), axes, 0, 0)


def dot(a, b, dims, **kw):
    return lax.dot_general(a, b, ((dims[:1], dims[1:]), ((), ())), preferred_element_type=jnp.float32, **kw)


def split3(v):
    hi = v.astype(jnp.bfloat16)
    rest = v - hi.astype(jnp.float32)
    mid = rest.astype(jnp.bfloat16)
    return [hi, mid, (rest - mid.astype(jnp.float32)).astype(jnp.bfloat16)]


def extra_rows(vec, scalars, rows):
    sc = jnp.concatenate([scalars, jnp.zeros((1, vec.shape[1] - scalars.shape[1]), jnp.float32)], axis=1)
    parts = [p.astype(jnp.float32) for p in split3(vec) + split3(sc)]
    parts.append(jnp.zeros((rows - 6, vec.shape[1]), jnp.float32))
    return jnp.concatenate(parts, axis=0).astype(jnp.bfloat16)


def join3(rows, n, at):
    return jnp.concatenate([r[n + 2 : n + 3, at] + r[n + 1 : n + 2, at] + r[n : n + 1, at] for r in rows], axis=0)


def pack_kernel(proj_ref, expr_ref, sums_ref, head_ref, out_ref):
    band, cells = proj_ref.shape
    genes = expr_ref.shape[1]
    cols = band // (N_FAR * N_NEAR)
    rows = N_FAR * cols
    proj = proj_ref[...]
    sums = sums_ref[...]
    proj_f = proj.astype(jnp.float32)
    w_col = jnp.sum(proj_f, axis=1, keepdims=True) / cells
    w_row = dot(jnp.ones((8, cells), jnp.bfloat16), proj, (1, 1))[:1] / cells
    quad = jnp.sum(proj_f * proj_f) - cells * jnp.sum(w_row * w_row)
    covar = dot(proj, expr_ref[...], (1, 0)) - w_col * sums
    mirror = covar[:, :band].T.astype(jnp.bfloat16)
    covar = covar.astype(jnp.bfloat16)
    lane = lax.broadcasted_iota(jnp.int32, head_ref.shape, 1)
    scalars = head_ref[...] + jnp.where(lane == 2, quad, 0.0)
    more = extra_rows(jnp.concatenate([sums / cells, w_row], axis=1), scalars, EXTRA)
    for k in range(N_NEAR):
        out_ref[k, :rows, :genes] = covar[k * rows : (k + 1) * rows]
        for h in range(N_FAR):
            at = (h * N_NEAR + k) * cols
            out_ref[k, h * cols : (h + 1) * cols, genes:] = mirror[at : at + cols]
        out_ref[k, rows:, :] = more


def merge(got, pick_a, pick_b, weight, genes, rows):
    n = got.shape[0]
    band = got.shape[2] - genes
    more = [got[i, rows:].astype(jnp.float32) for i in range(n)]
    vec = join3(more, 0, slice(None))
    mean = jnp.sum(vec, axis=0, keepdims=True) / n
    diff = vec - mean
    dm, dw = diff[:, :genes], diff[:, genes:]
    terms_w, terms_m = split3(dw), split3(dm[:, :band])
    left_a = sum(dot(t, pick_a, (1, 0)) for t in terms_w)
    left_b = sum(dot(t, pick_b, (1, 0)) for t in terms_m)
    high = lax.Precision.HIGHEST
    total = got[0, :rows].astype(jnp.float32)
    for i in range(1, n):
        total = total + got[i, :rows].astype(jnp.float32)
    total_a = total[:, :genes] + weight * dot(left_a, dm, (0, 0), precision=high)[:rows]
    total_b = total[:, genes:] + weight * dot(left_b, dw, (0, 0), precision=high)[:rows]
    sc = jnp.sum(join3(more, 3, slice(0, 128)), axis=0, keepdims=True)
    lane = lax.broadcasted_iota(jnp.int32, sc.shape, 1)
    sc = sc + jnp.where(lane == 2, weight * jnp.sum(dw * dw), 0.0)
    return total_a, total_b, mean, sc


def near_kernel(weight, genes, got_ref, pick_a_ref, pick_b_ref, out_ref, more_ref):
    rows = got_ref.shape[1] - EXTRA
    a, b, mean, sc = merge(got_ref[...], pick_a_ref[...], pick_b_ref[...], weight, genes, rows)
    a, b = a.astype(jnp.bfloat16), b.astype(jnp.bfloat16)
    cols = rows // N_FAR
    for h in range(N_FAR):
        out_ref[h, :, :genes] = a[h * cols : (h + 1) * cols]
        out_ref[h, :, genes:] = b[h * cols : (h + 1) * cols]
    more_ref[...] = extra_rows(mean, sc, EXTRA)


def far_kernel(weight, total, genes, place_ref, got_ref, pick_a_ref, pick_b_ref, order_ref, coef_ref, mirror_ref, out_ref, obj_ref):
    cols = coef_ref.shape[0]
    band = order_ref.shape[0]
    got = got_ref[...]
    a, b, _, sc = merge(got, pick_a_ref[...], pick_b_ref[...], weight, genes, cols)
    tile, part = place_ref[0], place_ref[1]
    coef = coef_ref[...]
    rows_id = lax.broadcasted_iota(jnp.int32, coef.shape, 1) + tile * genes
    cols_id = lax.broadcasted_iota(jnp.int32, coef.shape, 0) + part * cols
    on_diag = rows_id == cols_id
    inverse = jnp.where(on_diag, 1.0 / jnp.where(on_diag, coef, 1.0), 0.0)
    stepped = coef - STEP * (a / total - inverse)
    limit = STEP * PENALTY
    shrunk = jnp.where(on_diag, stepped, stepped - jnp.clip(stepped, -limit, limit))
    stepped_m = mirror_ref[...] - STEP * (b / total)
    shrunk_m = stepped_m - jnp.clip(stepped_m, -limit, limit)
    shrunk_m = sum(dot(t, order_ref[...], (1, 0)) for t in split3(shrunk_m)[:2])
    top = shrunk[:, :band]
    use = jnp.logical_and(tile == 0, jnp.logical_not(on_diag[:, :band]))
    out_ref[:, :band] = jnp.where(use, 0.5 * (top + shrunk_m), top)
    out_ref[:, band:] = shrunk[:, band:]
    lane = lax.broadcasted_iota(jnp.int32, sc.shape, 1)
    factor = jnp.where(lane == 0, -1.0, jnp.where(lane == 1, PENALTY, jnp.where(lane == 2, 1.0 / (2.0 * total), 0.0)))
    obj_ref[...] = jnp.sum(sc * factor, axis=1, keepdims=True)


def kernel(fn, outs, in_specs=None):
    specs = {} if in_specs is None else {"in_specs": in_specs}
    return pl.pallas_call(
        fn, out_shape=outs, compiler_params=pltpu.CompilerParams(vmem_limit_bytes=48 * 2**20), **specs
    )


def per_device(counts, coef):
    cells, genes = counts.shape
    cols = coef.shape[1]
    n_dp = N_FAR * N_NEAR
    band = cols * n_dp
    total = float(cells * n_dp)
    tile = lax.axis_index(TILE)
    near = lax.axis_index(NEAR)
    far = lax.axis_index(FAR)
    part = far * N_NEAR + near
    f32, bf16 = jnp.float32, jnp.bfloat16

    coef_t = coef.T
    w_far = spread(coef_t.astype(bf16), FAR, N_FAR).reshape(N_FAR * cols, genes)

    rows_id = lax.broadcasted_iota(jnp.int32, (cols, genes), 1) + tile * genes
    cols_id = lax.broadcasted_iota(jnp.int32, (cols, genes), 0) + part * cols
    on_diag = rows_id == cols_id
    safe = jnp.where(on_diag, coef_t, 1.0)
    logsum = jnp.sum(jnp.where(on_diag, jnp.log(safe), 0.0))
    absolute = jnp.sum(jnp.where(on_diag, 0.0, jnp.abs(coef_t)))

    lib_rows = cells // 128
    lib = jnp.sum(counts, axis=1).astype(f32).reshape(lib_rows, 128)
    sums = jnp.pad(jnp.stack([logsum, absolute])[None], ((0, 7 - lib_rows % 8), (0, 126)))
    head = lax.psum(lax.psum(jnp.concatenate([lib, sums]), "core"), "xl")
    w_far, head = lax.optimization_barrier((w_far, head))
    weights = spread(w_far, NEAR, N_NEAR).reshape(band, genes)
    head = lax.psum(head, "y")
    library = head[:lib_rows].reshape(cells)

    scale = SCALE / (library + 1.0)
    expr = jnp.log(1.0 + counts.astype(f32) * scale[:, None]).astype(bf16)
    expr = lax.optimization_barrier(expr)
    sums_e = jnp.sum(expr.astype(f32), axis=0, keepdims=True)

    partial = dot(weights, expr, (1, 1))
    got = lax.all_to_all(partial.astype(bf16).reshape(N_TILE, band // N_TILE, cells), TILE, 0, 0)
    mine = jnp.sum(got.astype(f32), axis=0).astype(bf16)
    proj = spread(mine, TILE, N_TILE).reshape(band, cells)

    rows = N_FAR * cols
    shape = jax.ShapeDtypeStruct((N_NEAR, rows + EXTRA, genes + band), bf16)
    got = kernel(pack_kernel, shape)(proj, expr, sums_e, head[lib_rows : lib_rows + 1])
    got = lax.all_to_all(got, NEAR, 0, 0)

    def onehot(at, n):
        return (lax.broadcasted_iota(jnp.int32, (n, at.shape[0]), 0) == at[None, :]).astype(bf16)

    slot = jnp.arange(rows, dtype=jnp.int32)
    pick_a = onehot(near * rows + slot, band)
    pick_b = onehot((slot // cols * N_NEAR + near) * cols + slot % cols, band)
    shapes = (
        jax.ShapeDtypeStruct((N_FAR, cols, genes + band), bf16),
        jax.ShapeDtypeStruct((EXTRA, genes + band), bf16),
    )
    main, more = kernel(functools.partial(near_kernel, float(cells), genes), shapes)(got, pick_a, pick_b)
    more = jnp.broadcast_to(more[None, :8], (N_FAR, 8, genes + band))
    got = lax.all_to_all(jnp.concatenate([main, more], axis=1), FAR, 0, 0)

    slot = jnp.arange(128, dtype=jnp.int32)
    slot_ok = slot < cols
    pick_a = onehot(jnp.where(slot_ok, near * rows + far * cols + slot, band), band)
    pick_b = onehot(jnp.where(slot_ok, part * cols + slot, band), band)
    nat = jnp.arange(band, dtype=jnp.int32)
    group = nat // cols
    order = onehot((group % N_NEAR * N_FAR + group // N_NEAR) * cols + nat % cols, band)
    here = onehot(part * cols + jnp.arange(cols, dtype=jnp.int32), genes)
    coef_m = dot(here, weights, (0, 1))
    place = jnp.stack([tile, part]).astype(jnp.int32)
    shapes = (jax.ShapeDtypeStruct((cols, genes), f32), jax.ShapeDtypeStruct((1, 1), f32))
    specs = [pl.BlockSpec(memory_space=pltpu.SMEM)] + [pl.BlockSpec(memory_space=pltpu.VMEM)] * 6
    new_t, objective = kernel(
        functools.partial(far_kernel, float(cells * N_NEAR), total, genes), shapes, specs
    )(place, got, pick_a, pick_b, order, coef_t, coef_m)
    return (new_t.T, objective[0, 0])


def solution(mesh):
    mesh = Mesh(mesh.devices.reshape(SIZES), AXES)
    return jax.shard_map(
        per_device,
        mesh=mesh,
        in_specs=(P((FAR,) + NEAR, TILE), P(TILE, (FAR,) + NEAR)),
        out_specs=(P(TILE, (FAR,) + NEAR), P()),
        check_vma=False,
    )
```

time: 185 us -> 166 us (0.90)
  other arithmetic: 22.6 us -> 9.19 us
  between operations: 7.34 us -> 0.75 us
  Pallas kernels: 0 us -> 5.87 us
  local copies, waits for them, and re-layouts: 7.9 us -> 2.82 us
  waiting for transfers between devices: 74.2 us -> 76.7 us
    convert_element_type x11 -> x3, other arithmetic: 6.85 us -> 0.27 us  [onehot(): (lax.broadcasted_iota(jnp.int32, (n, at.shape[0]), 0) == at[None, :]).ast...]
    pallas_call x0 -> x3, Pallas kernels: none -> 5.87 us  [the longest x1 2.45 us: per_device(): kernel(pack_kernel, shape)(proj, expr, sums_e, head[lib_rows:lib_rows + 1])]
    reduce_sum x15 -> x1, other arithmetic: 4.92 us -> 0.27 us  [per_device(): sums_e = jnp.sum(expr.astype(f32), axis=0, keepdims=True)]
where the time goes in v3:
time: 166 us
  waiting for transfers between devices  76.7 us (46%)
  starting transfers between devices  35.1 us (21%)
  blocking collectives  33.7 us (20%)
  other arithmetic  9.19 us (6%)
  Pallas kernels  5.87 us (4%)
  local copies, waits for them, and re-layouts  2.82 us (2%)
    all_to_all x1, waiting for transfers between devices, per_device(): got = lax.all_to_all(jnp.concatenate([main, more], axis=1), FAR, 0, 0)  33.1 us
    all_to_all x3, starting transfers between devices, spread(): lax.all_to_all(jnp.broadcast_to(block[None], (n,) + block.shape), axes, 0...  24.2 us
    all_to_all x1, waiting for transfers between devices, per_device(): got = lax.all_to_all(got, NEAR, 0, 0)  22.8 us
    all_to_all x3, waiting for transfers between devices, spread(): lax.all_to_all(jnp.broadcast_to(block[None], (n,) + block.shape), axes, 0...  20.9 us
    all_to_all x1, blocking collectives, per_device(): lax.all_to_all(partial.astype(bf16).reshape(N_TILE, band // N_TILE, cells...  15.6 us
    psum x1, blocking collectives, per_device(): head = lax.psum(head, 'y')  10.7 us
    psum x2, blocking collectives, per_device(): head = lax.psum(lax.psum(jnp.concatenate([lib, sums]), 'core'), 'xl')  7.39 us
    all_to_all x1, starting transfers between devices, per_device(): got = lax.all_to_all(got, NEAR, 0, 0)  5.89 us
  transfers between devices with their start and end apart: 5, of which 4 were waited for; matrix products, arithmetic and copies ran while one was open for 5% of the time, Pallas kernels for 0%

profile of v3, /device:TPU:32, one launch (start us, length us, event | category | flops | bytes accessed | tf_op | source)
XLA Modules:
  0.0 165.6 jit_solution(2615433112188887274)
XLA Ops:
  0.6 0.8 bitcast_convert_fusion
  2.2 14.3 %all-to-all-start = ((bf16[8,16,1024]{2,1,0:T(8,128)(2,1)}), bf16[8,16,1024]{2,1,0:T(8,128)(2,1)S(1)}, u32[]{:S(2)}, u32[]{:S(2)}) async-start(bf16[8,16,1024]{2,1,0:T(8,128)(2,1)} %broadcast_in_dim.25), calls=%async_computation | async-start | bytes 524288 | tf_op jit(solution)/shard_map/all_to_all | solution.py:24
  16.5 2.1 %reduce_sum.48 = s32[768]{0:T(1024)S(1)} reduce(s32[768,1024]{1,0:T(8,128)} %param.2, s32[]{:T(128)} %constant.105.clone.1), dimensions={1}, to_apply=%region_0.1 | reduce | flops 785664 | bytes 3148804 | tf_op jit(solution)/shard_map/reduce_sum | solution.py:164
  19.4 1.3 maximum_bitcast_fusion
  20.8 2.5 %psum.21 = f32[8,128]{1,0:T(8,128)S(1)} all-reduce(f32[8,128]{1,0:T(8,128)S(1)} %select_maximum_fusion), channel_id=1, replica_groups=mesh['zh'=8,'zl'=2,'xh'=2,'y'=4,'core'=2,'xl'=2] {'core'}, use_global_device_ids=true, to_apply=%region_3.4 | all-reduce | flops 1024 | bytes 8192 | tf_op jit(solution)/shard_map/psum | solution.py:166
  23.2 4.9 %psum.22 = f32[8,128]{1,0:T(8,128)S(1)} all-reduce(f32[8,128]{1,0:T(8,128)S(1)} %psum.21), channel_id=1, replica_groups=mesh['zh'=8,'zl'=2,'xh'=2,'y'=4,'core'=2,'xl'=2] {'xl'}, use_global_device_ids=true, to_apply=%region_4.5 | all-reduce | flops 1024 | bytes 8192 | tf_op jit(solution)/shard_map/psum | solution.py:166
  28.2 8.8 %all-to-all-done = bf16[8,16,1024]{2,1,0:T(8,128)(2,1)S(1)} async-done(((bf16[8,16,1024]{2,1,0:T(8,128)(2,1)}), bf16[8,16,1024]{2,1,0:T(8,128)(2,1)S(1)}, u32[]{:S(2)}, u32[]{:S(2)}) %all-to-all-start) | async-done | bytes 262176 | tf_op jit(solution)/shard_map/all_to_all | solution.py:24
  36.9 1.1 broadcast_in_dim.30
  38.0 6.3 %all-to-all-start.1 = ((bf16[4,128,1024]{2,1,0:T(8,128)(2,1)}), bf16[4,128,1024]{2,1,0:T(8,128)(2,1)S(1)}, u32[]{:S(2)}, u32[]{:S(2)}) async-start(bf16[4,128,1024]{2,1,0:T(8,128)(2,1)} %broadcast_in_dim.30), calls=%async_computation.1 | async-start | bytes 2097152 | tf_op jit(solution)/shard_map/all_to_all | solution.py:24
  44.3 10.7 %psum.23 = f32[8,128]{1,0:T(8,128)S(1)} all-reduce(f32[8,128]{1,0:T(8,128)S(1)} %psum.22), channel_id=1, replica_groups=mesh['zh'=8,'zl'=2,'xh'=2,'y'=4,'core'=2,'xl'=2] {'y'}, use_global_device_ids=true, to_apply=%region_5.6 | all-reduce | flops 1024 | bytes 8192 | tf_op jit(solution)/shard_map/psum | solution.py:169
  55.0 2.5 %log_convert_fusion.expr_ref = bf16[768,1024]{1,0:T(8,128)(2,1)S(1)} fusion(s32[768,1024]{1,0:T(8,128)} %param.2, f32[768]{0:T(1024)S(1)} %divide_bitcast_fusion), kind=kLoop, calls=%fused_computation.1 | loop fusion | flops 3145728 | bytes 4721664 | tf_op jit(solution)/shard_map/convert_element_type | solution.py:173
  57.6 1.0 convolution_convert_fusion
  58.6 15.6 %all_to_all.30 = bf16[16,32,768]{2,1,0:T(8,128)(2,1)S(1)} all-to-all(bf16[16,32,768]{2,1,0:T(8,128)(2,1)S(1)} %bitcast.30), channel_id=1, replica_groups=mesh['zh'=8,'zl'=2,'xh'=2,'y'=4,'core'=2,'xl'=2] {'y','core','xl'}, dimensions={0} | all-to-all | bytes 1572864 | tf_op jit(solution)/shard_map/all_to_all | solution.py:178
  74.3 1.0 broadcast_in_dim.56
  75.3 3.6 %all-to-all-start.3 = ((bf16[16,32,768]{2,1,0:T(8,128)(2,1)}), bf16[16,32,768]{2,1,0:T(8,128)(2,1)S(1)}, u32[]{:S(2)}, u32[]{:S(2)}) async-start(bf16[16,32,768]{2,1,0:T(8,128)(2,1)} %broadcast_in_dim.56), calls=%async_computation.3 | async-start | bytes 1572864 | tf_op jit(solution)/shard_map/all_to_all | solution.py:24
  79.2 12.1 %all-to-all-done.3 = bf16[16,32,768]{2,1,0:T(8,128)(2,1)S(1)} async-done(((bf16[16,32,768]{2,1,0:T(8,128)(2,1)}), bf16[16,32,768]{2,1,0:T(8,128)(2,1)S(1)}, u32[]{:S(2)}, u32[]{:S(2)}) %all-to-all-start.3) | async-done | bytes 786464 | tf_op jit(solution)/shard_map/all_to_all | solution.py:24
  91.3 2.5 %shard_map.41 = bf16[4,144,1536]{2,1,0:T(8,128)(2,1)} custom-call(bf16[512,768]{1,0:T(8,128)(2,1)S(1)} %bitcast.24, bf16[768,1024]{1,0:T(8,128)(2,1)S(1)} %log_convert_fusion.expr_ref, f32[1,1024]{1,0:T(1,128)S(1)} %bitcast.26, f32[1,128]{1,0:T(1,128)S(1)} %slice.10.head_ref), custom_call_target="tpu_custom_call" | custom-call | tf_op jit(solution)/shard_map/pallas_call | solution.py:184
  93.7 5.9 %all-to-all-start.4 = ((bf16[4,144,1536]{2,1,0:T(8,128)(2,1)}), bf16[4,144,1536]{2,1,0:T(8,128)(2,1)S(1)}, u32[]{:S(2)}, u32[]{:S(2)}) async-start(bf16[4,144,1536]{2,1,0:T(8,128)(2,1)} %shard_map.41), calls=%async_computation.4 | async-start | bytes 3538944 | tf_op jit(solution)/shard_map/all_to_all | solution.py:185
  99.7 22.8 %all-to-all-done.4.got_ref = bf16[4,144,1536]{2,1,0:T(8,128)(2,1)S(1)} async-done(((bf16[4,144,1536]{2,1,0:T(8,128)(2,1)}), bf16[4,144,1536]{2,1,0:T(8,128)(2,1)S(1)}, u32[]{:S(2)}, u32[]{:S(2)}) %all-to-all-start.4) | async-done | bytes 1769504 | tf_op jit(solution)/shard_map/all_to_all | solution.py:185
  122.5 1.0 shard_map.42
  123.5 0.8 pad_maximum_fusion
  124.4 5.0 %all-to-all-start.5 = ((bf16[8,24,1536]{2,1,0:T(8,128)(2,1)}), bf16[8,24,1536]{2,1,0:T(8,128)(2,1)S(1)}, u32[]{:S(2)}, u32[]{:S(2)}) async-start(bf16[8,24,1536]{2,1,0:T(8,128)(2,1)} %pad_maximum_fusion), calls=%async_computation.5 | async-start | bytes 1179648 | tf_op jit(solution)/shard_map/all_to_all | solution.py:199
  130.1 33.1 %all-to-all-done.5.got_ref = bf16[8,24,1536]{2,1,0:T(8,128)(2,1)S(1)} async-done(((bf16[8,24,1536]{2,1,0:T(8,128)(2,1)}), bf16[8,24,1536]{2,1,0:T(8,128)(2,1)S(1)}, u32[]{:S(2)}, u32[]{:S(2)}) %all-to-all-start.5) | async-done | bytes 589856 | tf_op jit(solution)/shard_map/all_to_all | solution.py:199
  163.2 2.4 %shard_map.43 = (f32[16,1024]{1,0:T(8,128)}, f32[1,1]{1,0:T(1,128)}) custom-call(s32[2]{0:T(128)S(1)} %pad_add_fusion.place_ref, bf16[8,24,1536]{2,1,0:T(8,128)(2,1)S(1)} %all-to-all-done.5.got_ref, bf16[512,128]{1,0:T(8,128)(2,1)S(1)} %get-tuple-element.18.pick_a_ref, bf16[512,128]{1,0:T(8,128)(2,1)S(1)} %get-tuple-element.19.pick_b_ref, ...), custom_call_target="tpu_custom_call" | custom-call | tf_op jit(solution)/shard_map/pallas_call | solution.py:213
  (25 shorter events, 2.7 us)
Async XLA Ops:
  2.2 16.5 %copy-start = (f32[1024,16]{0,1:T(8,128)S(1)}, f32[1024,16]{0,1:T(8,128)}, u32[]{:S(2)}) copy-start(f32[1024,16]{0,1:T(8,128)} %param.3) | copy-start | bytes 196612
  2.2 34.7 %all-to-all-start = ((bf16[8,16,1024]{2,1,0:T(8,128)(2,1)}), bf16[8,16,1024]{2,1,0:T(8,128)(2,1)S(1)}, u32[]{:S(2)}, u32[]{:S(2)}) async-start(bf16[8,16,1024]{2,1,0:T(8,128)(2,1)} %broadcast_in_dim.25), calls=%async_computation | async-start | bytes 524288 | tf_op jit(solution)/shard_map/all_to_all | solution.py:24
  38.0 19.5 %all-to-all-start.1 = ((bf16[4,128,1024]{2,1,0:T(8,128)(2,1)}), bf16[4,128,1024]{2,1,0:T(8,128)(2,1)S(1)}, u32[]{:S(2)}, u32[]{:S(2)}) async-start(bf16[4,128,1024]{2,1,0:T(8,128)(2,1)} %broadcast_in_dim.30), calls=%async_computation.1 | async-start | bytes 2097152 | tf_op jit(solution)/shard_map/all_to_all | solution.py:24
  75.3 16.0 %all-to-all-start.3 = ((bf16[16,32,768]{2,1,0:T(8,128)(2,1)}), bf16[16,32,768]{2,1,0:T(8,128)(2,1)S(1)}, u32[]{:S(2)}, u32[]{:S(2)}) async-start(bf16[16,32,768]{2,1,0:T(8,128)(2,1)} %broadcast_in_dim.56), calls=%async_computation.3 | async-start | bytes 1572864 | tf_op jit(solution)/shard_map/all_to_all | solution.py:24
  93.7 28.7 %all-to-all-start.4 = ((bf16[4,144,1536]{2,1,0:T(8,128)(2,1)}), bf16[4,144,1536]{2,1,0:T(8,128)(2,1)S(1)}, u32[]{:S(2)}, u32[]{:S(2)}) async-start(bf16[4,144,1536]{2,1,0:T(8,128)(2,1)} %shard_map.41), calls=%async_computation.4 | async-start | bytes 3538944 | tf_op jit(solution)/shard_map/all_to_all | solution.py:185
  124.4 38.8 %all-to-all-start.5 = ((bf16[8,24,1536]{2,1,0:T(8,128)(2,1)}), bf16[8,24,1536]{2,1,0:T(8,128)(2,1)S(1)}, u32[]{:S(2)}, u32[]{:S(2)}) async-start(bf16[8,24,1536]{2,1,0:T(8,128)(2,1)} %pad_maximum_fusion), calls=%async_computation.5 | async-start | bytes 1179648 | tf_op jit(solution)/shard_map/all_to_all | solution.py:199

commit v4 on v3

--- a/solution.py
+++ b/solution.py
@@ -17,7 +17,7 @@
 AXES = (FAR,) + NEAR + TILE
 SIZES = (8, 2, 2, 4, 2, 2)
 N_FAR, N_NEAR, N_TILE = 8, 4, 16
-EXTRA = 16
+LANES = 128
 
 
 def spread(block, axes, n):
@@ -35,15 +35,21 @@
     return [hi, mid, (rest - mid.astype(jnp.float32)).astype(jnp.bfloat16)]
 
 
-def extra_rows(vec, scalars, rows):
-    sc = jnp.concatenate([scalars, jnp.zeros((1, vec.shape[1] - scalars.shape[1]), jnp.float32)], axis=1)
-    parts = [p.astype(jnp.float32) for p in split3(vec) + split3(sc)]
-    parts.append(jnp.zeros((rows - 6, vec.shape[1]), jnp.float32))
-    return jnp.concatenate(parts, axis=0).astype(jnp.bfloat16)
-
-
-def join3(rows, n, at):
-    return jnp.concatenate([r[n + 2 : n + 3, at] + r[n + 1 : n + 2, at] + r[n : n + 1, at] for r in rows], axis=0)
+def extra_rows(vec, scalars):
+    terms = [t.astype(jnp.float32) for t in split3(vec)[:2]]
+    rows = [t[:, i : i + LANES] for t in terms for i in range(0, vec.shape[1], LANES)]
+    return rows + [t.astype(jnp.float32) for t in split3(scalars)]
+
+
+def join_rows(row, n):
+    vec = jnp.concatenate([row(n + i) + row(i) for i in range(n)], axis=1)
+    return vec, row(2 * n + 2) + row(2 * n + 1) + row(2 * n)
+
+
+def spread_kernel(block_ref, out_ref):
+    block = block_ref[...].astype(jnp.bfloat16)
+    for i in range(out_ref.shape[0]):
+        out_ref[i] = block
 
 
 def pack_kernel(proj_ref, expr_ref, sums_ref, head_ref, out_ref):
@@ -62,20 +68,19 @@
     covar = covar.astype(jnp.bfloat16)
     lane = lax.broadcasted_iota(jnp.int32, head_ref.shape, 1)
     scalars = head_ref[...] + jnp.where(lane == 2, quad, 0.0)
-    more = extra_rows(jnp.concatenate([sums / cells, w_row], axis=1), scalars, EXTRA)
+    more = extra_rows(jnp.concatenate([sums / cells, w_row], axis=1), scalars)
+    more.append(jnp.zeros((rows - len(more), LANES), jnp.float32))
+    more = jnp.concatenate(more, axis=0).astype(jnp.bfloat16)
     for k in range(N_NEAR):
-        out_ref[k, :rows, :genes] = covar[k * rows : (k + 1) * rows]
+        out_ref[k, :, :genes] = covar[k * rows : (k + 1) * rows]
         for h in range(N_FAR):
             at = (h * N_NEAR + k) * cols
-            out_ref[k, h * cols : (h + 1) * cols, genes:] = mirror[at : at + cols]
-        out_ref[k, rows:, :] = more
-
-
-def merge(got, pick_a, pick_b, weight, genes, rows):
-    n = got.shape[0]
-    band = got.shape[2] - genes
-    more = [got[i, rows:].astype(jnp.float32) for i in range(n)]
-    vec = join3(more, 0, slice(None))
+            out_ref[k, h * cols : (h + 1) * cols, genes : genes + band] = mirror[at : at + cols]
+        out_ref[k, :, genes + band :] = more
+
+
+def merge(got, vec, sc, pick_a, pick_b, weight, genes, band):
+    n, rows = got.shape[:2]
     mean = jnp.sum(vec, axis=0, keepdims=True) / n
     diff = vec - mean
     dm, dw = diff[:, :genes], diff[:, genes:]
@@ -83,33 +88,48 @@
     left_a = sum(dot(t, pick_a, (1, 0)) for t in terms_w)
     left_b = sum(dot(t, pick_b, (1, 0)) for t in terms_m)
     high = lax.Precision.HIGHEST
-    total = got[0, :rows].astype(jnp.float32)
+    total = got[0, :, : genes + band].astype(jnp.float32)
     for i in range(1, n):
-        total = total + got[i, :rows].astype(jnp.float32)
+        total = total + got[i, :, : genes + band].astype(jnp.float32)
     total_a = total[:, :genes] + weight * dot(left_a, dm, (0, 0), precision=high)[:rows]
     total_b = total[:, genes:] + weight * dot(left_b, dw, (0, 0), precision=high)[:rows]
-    sc = jnp.sum(join3(more, 3, slice(0, 128)), axis=0, keepdims=True)
+    sc = jnp.sum(sc, axis=0, keepdims=True)
     lane = lax.broadcasted_iota(jnp.int32, sc.shape, 1)
     sc = sc + jnp.where(lane == 2, weight * jnp.sum(dw * dw), 0.0)
     return total_a, total_b, mean, sc
 
 
-def near_kernel(weight, genes, got_ref, pick_a_ref, pick_b_ref, out_ref, more_ref):
-    rows = got_ref.shape[1] - EXTRA
-    a, b, mean, sc = merge(got_ref[...], pick_a_ref[...], pick_b_ref[...], weight, genes, rows)
+def near_kernel(weight, genes, got_ref, pick_a_ref, pick_b_ref, out_ref):
+    n, rows, wide = got_ref.shape
+    both = wide - LANES
+    got = got_ref[...]
+    more = [got[i, :32, both:].astype(jnp.float32) for i in range(n)]
+    vec, sc = join_rows(lambda r: jnp.concatenate([m[r : r + 1] for m in more], axis=0), both // LANES)
+    a, b, mean, sc = merge(got, vec, sc, pick_a_ref[...], pick_b_ref[...], weight, genes, both - genes)
     a, b = a.astype(jnp.bfloat16), b.astype(jnp.bfloat16)
     cols = rows // N_FAR
+    more = extra_rows(mean, sc)
+    more += [jnp.zeros((1, LANES), jnp.float32)] * (2 * cols - len(more))
+    more = [jnp.concatenate(more[i : i + cols], axis=0).astype(jnp.bfloat16) for i in (0, cols)]
     for h in range(N_FAR):
         out_ref[h, :, :genes] = a[h * cols : (h + 1) * cols]
-        out_ref[h, :, genes:] = b[h * cols : (h + 1) * cols]
-    more_ref[...] = extra_rows(mean, sc, EXTRA)
+        out_ref[h, :, genes:both] = b[h * cols : (h + 1) * cols]
+        out_ref[h, :, both : both + LANES] = more[0]
+        out_ref[h, :, both + LANES :] = more[1]
 
 
 def far_kernel(weight, total, genes, place_ref, got_ref, pick_a_ref, pick_b_ref, order_ref, coef_ref, mirror_ref, out_ref, obj_ref):
     cols = coef_ref.shape[0]
     band = order_ref.shape[0]
     got = got_ref[...]
-    a, b, _, sc = merge(got, pick_a_ref[...], pick_b_ref[...], weight, genes, cols)
+    more = got[:, :, genes + band :].astype(jnp.float32)
+
+    def row(i):
+        at = i // cols * LANES
+        return more[:, i % cols, at : at + LANES]
+
+    vec, sc = join_rows(row, (genes + band) // LANES)
+    a, b, _, sc = merge(got, vec, sc, pick_a_ref[...], pick_b_ref[...], weight, genes, band)
     tile, part = place_ref[0], place_ref[1]
     coef = coef_ref[...]
     rows_id = lax.broadcasted_iota(jnp.int32, coef.shape, 1) + tile * genes
@@ -151,7 +171,8 @@
     f32, bf16 = jnp.float32, jnp.bfloat16
 
     coef_t = coef.T
-    w_far = spread(coef_t.astype(bf16), FAR, N_FAR).reshape(N_FAR * cols, genes)
+    w_far = kernel(spread_kernel, jax.ShapeDtypeStruct((N_FAR, cols, genes), bf16))(coef_t)
+    w_far = lax.all_to_all(w_far, FAR, 0, 0).reshape(N_FAR * cols, genes)
 
     rows_id = lax.broadcasted_iota(jnp.int32, (cols, genes), 1) + tile * genes
     cols_id = lax.broadcasted_iota(jnp.int32, (cols, genes), 0) + part * cols
@@ -180,7 +201,7 @@
     proj = spread(mine, TILE, N_TILE).reshape(band, cells)
 
     rows = N_FAR * cols
-    shape = jax.ShapeDtypeStruct((N_NEAR, rows + EXTRA, genes + band), bf16)
+    shape = jax.ShapeDtypeStruct((N_NEAR, rows, genes + band + LANES), bf16)
     got = kernel(pack_kernel, shape)(proj, expr, sums_e, head[lib_rows : lib_rows + 1])
     got = lax.all_to_all(got, NEAR, 0, 0)
 
@@ -190,15 +211,11 @@
     slot = jnp.arange(rows, dtype=jnp.int32)
     pick_a = onehot(near * rows + slot, band)
     pick_b = onehot((slot // cols * N_NEAR + near) * cols + slot % cols, band)
-    shapes = (
-        jax.ShapeDtypeStruct((N_FAR, cols, genes + band), bf16),
-        jax.ShapeDtypeStruct((EXTRA, genes + band), bf16),
-    )
-    main, more = kernel(functools.partial(near_kernel, float(cells), genes), shapes)(got, pick_a, pick_b)
-    more = jnp.broadcast_to(more[None, :8], (N_FAR, 8, genes + band))
-    got = lax.all_to_all(jnp.concatenate([main, more], axis=1), FAR, 0, 0)
-
-    slot = jnp.arange(128, dtype=jnp.int32)
+    shape = jax.ShapeDtypeStruct((N_FAR, cols, genes + band + 2 * LANES), bf16)
+    got = kernel(functools.partial(near_kernel, float(cells), genes), shape)(got, pick_a, pick_b)
+    got = lax.all_to_all(got, FAR, 0, 0)
+
+    slot = jnp.arange(LANES, dtype=jnp.int32)
     slot_ok = slot < cols
     pick_a = onehot(jnp.where(slot_ok, near * rows + far * cols + slot, band), band)
     pick_b = onehot(jnp.where(slot_ok, part * cols + slot, band), band)

time: 166 us -> 160 us (0.964)
  the two profiles are of different devices: /device:TPU:32 before, /device:TPU:6 now
where the time goes in v4:
time: 160 us; the launch traced here: 159 us
  waiting for transfers between devices  70.2 us (44%)
  starting transfers between devices  35.4 us (22%)
  blocking collectives  33.9 us (21%)
  other arithmetic  7.5 us (5%)
  Pallas kernels  7.32 us (5%)
  local copies, waits for them, and re-layouts  2.92 us (2%)
    all_to_all x1, waiting for transfers between devices, per_device(): got = lax.all_to_all(got, FAR, 0, 0)  28.1 us
    all_to_all x1, waiting for transfers between devices, per_device(): got = lax.all_to_all(got, NEAR, 0, 0)  20.6 us
    all_to_all x1, blocking collectives, per_device(): lax.all_to_all(partial.astype(bf16).reshape(N_TILE, band // N_TILE, cells...  15.8 us
    all_to_all x1, starting transfers between devices, per_device(): w_far = lax.all_to_all(w_far, FAR, 0, 0).reshape(N_FAR * cols, genes)  15.1 us
    all_to_all x2, waiting for transfers between devices, spread(): lax.all_to_all(jnp.broadcast_to(block[None], (n,) + block.shape), axes, 0...  11.8 us
    psum x1, blocking collectives, per_device(): head = lax.psum(head, 'y')  10.7 us
    all_to_all x1, waiting for transfers between devices, per_device(): w_far = lax.all_to_all(w_far, FAR, 0, 0).reshape(N_FAR * cols, genes)  9.73 us
    all_to_all x2, starting transfers between devices, spread(): lax.all_to_all(jnp.broadcast_to(block[None], (n,) + block.shape), axes, 0...  9 us
  transfers between devices with their start and end apart: 5, of which 4 were waited for; matrix products, arithmetic and copies ran while one was open for 5% of the time, Pallas kernels for 0%

profile of v4, /device:TPU:6, one launch (start us, length us, event | category | flops | bytes accessed | tf_op | source)
XLA Modules:
  0.0 159.4 jit_solution(17616011068270758395)
XLA Ops:
  0.6 0.8 copy-done
  2.2 15.1 %all-to-all-start = ((bf16[8,16,1024]{2,1,0:T(8,128)(2,1)}), bf16[8,16,1024]{2,1,0:T(8,128)(2,1)S(1)}, u32[]{:S(2)}, u32[]{:S(2)}) async-start(bf16[8,16,1024]{2,1,0:T(8,128)(2,1)} %shard_map.41), calls=%async_computation | async-start | bytes 524288 | tf_op jit(solution)/shard_map/all_to_all | solution.py:175
  17.3 2.1 %reduce_sum.48 = s32[768]{0:T(1024)S(1)} reduce(s32[768,1024]{1,0:T(8,128)} %param.2, s32[]{:T(128)} %constant.105.clone.1), dimensions={1}, to_apply=%region_0.1 | reduce | flops 785664 | bytes 3148804 | tf_op jit(solution)/shard_map/reduce_sum | solution.py:185
  19.4 0.8 fusion.10
  20.2 1.3 maximum_bitcast_fusion
  21.5 2.5 %psum.21 = f32[8,128]{1,0:T(8,128)S(1)} all-reduce(f32[8,128]{1,0:T(8,128)S(1)} %select_maximum_fusion), channel_id=1, replica_groups=mesh['zh'=8,'zl'=2,'xh'=2,'y'=4,'core'=2,'xl'=2] {'core'}, use_global_device_ids=true, to_apply=%region_3.4 | all-reduce | flops 1024 | bytes 8192 | tf_op jit(solution)/shard_map/psum | solution.py:187
  24.0 4.9 %psum.22 = f32[8,128]{1,0:T(8,128)S(1)} all-reduce(f32[8,128]{1,0:T(8,128)S(1)} %psum.21), channel_id=1, replica_groups=mesh['zh'=8,'zl'=2,'xh'=2,'y'=4,'core'=2,'xl'=2] {'xl'}, use_global_device_ids=true, to_apply=%region_4.5 | all-reduce | flops 1024 | bytes 8192 | tf_op jit(solution)/shard_map/psum | solution.py:187
  28.9 9.7 %all-to-all-done = bf16[8,16,1024]{2,1,0:T(8,128)(2,1)S(1)} async-done(((bf16[8,16,1024]{2,1,0:T(8,128)(2,1)}), bf16[8,16,1024]{2,1,0:T(8,128)(2,1)S(1)}, u32[]{:S(2)}, u32[]{:S(2)}) %all-to-all-start) | async-done | bytes 262176 | tf_op jit(solution)/shard_map/all_to_all | solution.py:175
  38.6 1.1 broadcast_in_dim.42
  39.8 4.9 %all-to-all-start.1 = ((bf16[4,128,1024]{2,1,0:T(8,128)(2,1)}), bf16[4,128,1024]{2,1,0:T(8,128)(2,1)S(1)}, u32[]{:S(2)}, u32[]{:S(2)}) async-start(bf16[4,128,1024]{2,1,0:T(8,128)(2,1)} %broadcast_in_dim.42), calls=%async_computation.1 | async-start | bytes 2097152 | tf_op jit(solution)/shard_map/all_to_all | solution.py:24
  44.7 10.7 %psum.23 = f32[8,128]{1,0:T(8,128)S(1)} all-reduce(f32[8,128]{1,0:T(8,128)S(1)} %psum.22), channel_id=1, replica_groups=mesh['zh'=8,'zl'=2,'xh'=2,'y'=4,'core'=2,'xl'=2] {'y'}, use_global_device_ids=true, to_apply=%region_5.6 | all-reduce | flops 1024 | bytes 8192 | tf_op jit(solution)/shard_map/psum | solution.py:190
  55.4 2.5 %log_convert_fusion.expr_ref = bf16[768,1024]{1,0:T(8,128)(2,1)S(1)} fusion(s32[768,1024]{1,0:T(8,128)} %param.2, f32[768]{0:T(1024)S(1)} %divide_bitcast_fusion), kind=kLoop, calls=%fused_computation.1 | loop fusion | flops 3145728 | bytes 4721664 | tf_op jit(solution)/shard_map/convert_element_type | solution.py:194
  57.9 1.0 convolution_convert_fusion
  58.9 15.8 %all_to_all.30 = bf16[16,32,768]{2,1,0:T(8,128)(2,1)S(1)} all-to-all(bf16[16,32,768]{2,1,0:T(8,128)(2,1)S(1)} %bitcast.30), channel_id=1, replica_groups=mesh['zh'=8,'zl'=2,'xh'=2,'y'=4,'core'=2,'xl'=2] {'y','core','xl'}, dimensions={0} | all-to-all | bytes 1572864 | tf_op jit(solution)/shard_map/all_to_all | solution.py:199
  74.9 1.0 broadcast_in_dim.43
  75.8 4.1 %all-to-all-start.3 = ((bf16[16,32,768]{2,1,0:T(8,128)(2,1)}), bf16[16,32,768]{2,1,0:T(8,128)(2,1)S(1)}, u32[]{:S(2)}, u32[]{:S(2)}) async-start(bf16[16,32,768]{2,1,0:T(8,128)(2,1)} %broadcast_in_dim.43), calls=%async_computation.3 | async-start | bytes 1572864 | tf_op jit(solution)/shard_map/all_to_all | solution.py:24
  80.2 11.8 %all-to-all-done.3 = bf16[16,32,768]{2,1,0:T(8,128)(2,1)S(1)} async-done(((bf16[16,32,768]{2,1,0:T(8,128)(2,1)}), bf16[16,32,768]{2,1,0:T(8,128)(2,1)S(1)}, u32[]{:S(2)}, u32[]{:S(2)}) %all-to-all-start.3) | async-done | bytes 786464 | tf_op jit(solution)/shard_map/all_to_all | solution.py:24
  92.0 2.4 %shard_map.42 = bf16[4,128,1664]{2,1,0:T(8,128)(2,1)} custom-call(bf16[512,768]{1,0:T(8,128)(2,1)S(1)} %bitcast.23, bf16[768,1024]{1,0:T(8,128)(2,1)S(1)} %log_convert_fusion.expr_ref, f32[1,1024]{1,0:T(1,128)S(1)} %bitcast.26, f32[1,128]{1,0:T(1,128)S(1)} %slice.7.head_ref), custom_call_target="tpu_custom_call" | custom-call | tf_op jit(solution)/shard_map/pallas_call | solution.py:205
  94.4 5.7 %all-to-all-start.4 = ((bf16[4,128,1664]{2,1,0:T(8,128)(2,1)}), bf16[4,128,1664]{2,1,0:T(8,128)(2,1)S(1)}, u32[]{:S(2)}, u32[]{:S(2)}) async-start(bf16[4,128,1664]{2,1,0:T(8,128)(2,1)} %shard_map.42), calls=%async_computation.4 | async-start | bytes 3407872 | tf_op jit(solution)/shard_map/all_to_all | solution.py:206
  100.2 20.6 %all-to-all-done.4.got_ref = bf16[4,128,1664]{2,1,0:T(8,128)(2,1)S(1)} async-done(((bf16[4,128,1664]{2,1,0:T(8,128)(2,1)}), bf16[4,128,1664]{2,1,0:T(8,128)(2,1)S(1)}, u32[]{:S(2)}, u32[]{:S(2)}) %all-to-all-start.4) | async-done | bytes 1703968 | tf_op jit(solution)/shard_map/all_to_all | solution.py:206
  120.8 1.8 %shard_map.43 = bf16[8,16,1792]{2,1,0:T(8,128)(2,1)} custom-call(bf16[4,128,1664]{2,1,0:T(8,128)(2,1)S(1)} %all-to-all-done.4.got_ref, bf16[512,128]{1,0:T(8,128)(2,1)S(1)} %get-tuple-element.12.pick_a_ref, bf16[512,128]{1,0:T(8,128)(2,1)S(1)} %get-tuple-element.13.pick_b_ref), custom_call_target="tpu_custom_call" | custom-call | tf_op jit(solution)/shard_map/pallas_call | solution.py:215
  122.6 5.6 %all-to-all-start.5 = ((bf16[8,16,1792]{2,1,0:T(8,128)(2,1)}), bf16[8,16,1792]{2,1,0:T(8,128)(2,1)S(1)}, u32[]{:S(2)}, u32[]{:S(2)}) async-start(bf16[8,16,1792]{2,1,0:T(8,128)(2,1)} %shard_map.43), calls=%async_computation.5 | async-start | bytes 917504 | tf_op jit(solution)/shard_map/all_to_all | solution.py:216
  128.9 28.1 %all-to-all-done.5.got_ref = bf16[8,16,1792]{2,1,0:T(8,128)(2,1)S(1)} async-done(((bf16[8,16,1792]{2,1,0:T(8,128)(2,1)}), bf16[8,16,1792]{2,1,0:T(8,128)(2,1)S(1)}, u32[]{:S(2)}, u32[]{:S(2)}) %all-to-all-start.5) | async-done | bytes 458784 | tf_op jit(solution)/shard_map/all_to_all | solution.py:216
  157.0 2.4 %shard_map.44 = (f32[16,1024]{1,0:T(8,128)}, f32[1,1]{1,0:T(1,128)}) custom-call(s32[2]{0:T(128)S(1)} %pad_add_fusion.place_ref, bf16[8,16,1792]{2,1,0:T(8,128)(2,1)S(1)} %all-to-all-done.5.got_ref, bf16[512,128]{1,0:T(8,128)(2,1)S(1)} %get-tuple-element.14.pick_a_ref, bf16[512,128]{1,0:T(8,128)(2,1)S(1)} %get-tuple-element.15.pick_b_ref, ...), custom_call_target="tpu_custom_call" | custom-call | tf_op jit(solution)/shard_map/pallas_call | solution.py:230
  (23 shorter events, 1.9 us)
Async XLA Ops:
  0.6 0.8 copy-start
  1.5 17.9 %copy-start.1 = (f32[1024,16]{0,1:T(8,128)S(1)}, f32[1024,16]{0,1:T(8,128)}, u32[]{:S(2)}) copy-start(f32[1024,16]{0,1:T(8,128)} %param.3) | copy-start | bytes 196612
  2.2 36.5 %all-to-all-start = ((bf16[8,16,1024]{2,1,0:T(8,128)(2,1)}), bf16[8,16,1024]{2,1,0:T(8,128)(2,1)S(1)}, u32[]{:S(2)}, u32[]{:S(2)}) async-start(bf16[8,16,1024]{2,1,0:T(8,128)(2,1)} %shard_map.41), calls=%async_computation | async-start | bytes 524288 | tf_op jit(solution)/shard_map/all_to_all | solution.py:175
  39.8 18.1 %all-to-all-start.1 = ((bf16[4,128,1024]{2,1,0:T(8,128)(2,1)}), bf16[4,128,1024]{2,1,0:T(8,128)(2,1)S(1)}, u32[]{:S(2)}, u32[]{:S(2)}) async-start(bf16[4,128,1024]{2,1,0:T(8,128)(2,1)} %broadcast_in_dim.42), calls=%async_computation.1 | async-start | bytes 2097152 | tf_op jit(solution)/shard_map/all_to_all | solution.py:24
  75.8 16.2 %all-to-all-start.3 = ((bf16[16,32,768]{2,1,0:T(8,128)(2,1)}), bf16[16,32,768]{2,1,0:T(8,128)(2,1)S(1)}, u32[]{:S(2)}, u32[]{:S(2)}) async-start(bf16[16,32,768]{2,1,0:T(8,128)(2,1)} %broadcast_in_dim.43), calls=%async_computation.3 | async-start | bytes 1572864 | tf_op jit(solution)/shard_map/all_to_all | solution.py:24
  94.4 26.4 %all-to-all-start.4 = ((bf16[4,128,1664]{2,1,0:T(8,128)(2,1)}), bf16[4,128,1664]{2,1,0:T(8,128)(2,1)S(1)}, u32[]{:S(2)}, u32[]{:S(2)}) async-start(bf16[4,128,1664]{2,1,0:T(8,128)(2,1)} %shard_map.42), calls=%async_computation.4 | async-start | bytes 3407872 | tf_op jit(solution)/shard_map/all_to_all | solution.py:206
  122.6 34.4 %all-to-all-start.5 = ((bf16[8,16,1792]{2,1,0:T(8,128)(2,1)}), bf16[8,16,1792]{2,1,0:T(8,128)(2,1)S(1)}, u32[]{:S(2)}, u32[]{:S(2)}) async-start(bf16[8,16,1792]{2,1,0:T(8,128)(2,1)} %shard_map.43), calls=%async_computation.5 | async-start | bytes 917504 | tf_op jit(solution)/shard_map/all_to_all | solution.py:216

commit v5 on v4

v5 whole, which is shorter than its diff:
```python
import functools

import jax
import jax.numpy as jnp
from jax import lax
from jax.experimental import pallas as pl
from jax.experimental.pallas import tpu as pltpu
from jax.sharding import Mesh, PartitionSpec as P

STEP = 0.5
PENALTY = 0.05
SCALE = 10000.0

FAR = "zh"
NEAR = ("zl", "xh")
TILE = ("y", "core", "xl")
AXES = (FAR,) + NEAR + TILE
SIZES = (8, 2, 2, 4, 2, 2)
N_FAR, N_NEAR, N_TILE = 8, 4, 16
LANES = 128


def dot(a, b, dims, **kw):
    return lax.dot_general(a, b, ((dims[:1], dims[1:]), ((), ())), preferred_element_type=jnp.float32, **kw)


def split3(v):
    hi = v.astype(jnp.bfloat16)
    rest = v - hi.astype(jnp.float32)
    mid = rest.astype(jnp.bfloat16)
    return [hi, mid, (rest - mid.astype(jnp.float32)).astype(jnp.bfloat16)]


def extra_rows(vec, scalars):
    terms = [t.astype(jnp.float32) for t in split3(vec)[:2]]
    rows = [t[:, i : i + LANES] for t in terms for i in range(0, vec.shape[1], LANES)]
    return rows + [t.astype(jnp.float32) for t in split3(scalars)]


def join_rows(row, n):
    vec = jnp.concatenate([row(n + i) + row(i) for i in range(n)], axis=1)
    return vec, row(2 * n + 2) + row(2 * n + 1) + row(2 * n)


def spread_kernel(block_ref, out_ref):
    block = block_ref[...]
    if block.ndim == 3:
        block = jnp.sum(block.astype(jnp.float32), axis=0)
    block = block.astype(jnp.bfloat16)
    for i in range(out_ref.shape[0]):
        out_ref[i] = block


def pack_kernel(mirrored, proj_ref, expr_ref, sums_ref, head_ref, out_ref):
    band, cells = proj_ref.shape
    genes = expr_ref.shape[1]
    cols = band // (N_FAR * N_NEAR)
    rows = N_FAR * cols
    proj = proj_ref[...]
    sums = sums_ref[...]
    proj_f = proj.astype(jnp.float32)
    w_col = jnp.sum(proj_f, axis=1, keepdims=True) / cells
    w_row = dot(jnp.ones((8, cells), jnp.bfloat16), proj, (1, 1))[:1] / cells
    quad = jnp.sum(proj_f * proj_f) - cells * jnp.sum(w_row * w_row)
    covar = dot(proj, expr_ref[...], (1, 0)) - w_col * sums
    if mirrored:
        mirror = covar[:, :band].T.astype(jnp.bfloat16)
    covar = covar.astype(jnp.bfloat16)
    lane = lax.broadcasted_iota(jnp.int32, head_ref.shape, 1)
    scalars = head_ref[...] + jnp.where(lane == 2, quad, 0.0)
    more = extra_rows(jnp.concatenate([sums / cells, w_row], axis=1), scalars)
    more.append(jnp.zeros((rows - len(more), LANES), jnp.float32))
    more = jnp.concatenate(more, axis=0).astype(jnp.bfloat16)
    for k in range(N_NEAR):
        out_ref[k, :, :genes] = covar[k * rows : (k + 1) * rows]
        out_ref[k, :, genes : genes + LANES] = more
        if mirrored:
            for h in range(N_FAR):
                at = (h * N_NEAR + k) * cols
                out_ref[k, h * cols : (h + 1) * cols, genes + LANES :] = mirror[at : at + cols]


def merge(got, vec, sc, picks, weight, genes, band):
    n, rows, wide = got.shape
    mean = jnp.sum(vec, axis=0, keepdims=True) / n
    diff = vec - mean
    dm, dw = diff[:, :genes], diff[:, genes:]

    def total(part, left, right, pick):
        left = sum(dot(t, pick, (1, 0)) for t in split3(left))
        out = sum(part[i].astype(jnp.float32) for i in range(n))
        return out + weight * dot(left, right, (0, 0), precision=lax.Precision.HIGHEST)

    totals = [total(got[:, :, :genes], dw, dm, picks[0])]
    if len(picks) == 2:
        totals.append(total(got[:, :, wide - band :], dm[:, :band], dw, picks[1]))
    sc = jnp.sum(sc, axis=0, keepdims=True)
    lane = lax.broadcasted_iota(jnp.int32, sc.shape, 1)
    sc = sc + jnp.where(lane == 2, weight * jnp.sum(dw * dw), 0.0)
    return totals, mean, sc


def near_kernel(weight, genes, got_ref, *refs):
    n, rows, wide = got_ref.shape
    picks, out_ref = [r[...] for r in refs[:-1]], refs[-1]
    band = picks[0].shape[0]
    cols = rows // N_FAR
    got = got_ref[...]
    more = [got[i, :32, genes : genes + LANES].astype(jnp.float32) for i in range(n)]
    vec, sc = join_rows(lambda r: jnp.concatenate([m[r : r + 1] for m in more], axis=0), (genes + band) // LANES)
    totals, mean, sc = merge(got, vec, sc, picks, weight, genes, band)
    more = extra_rows(mean, sc)
    more += [jnp.zeros((1, LANES), jnp.float32)] * (2 * cols - len(more))
    more = [jnp.concatenate(more[i : i + cols], axis=0).astype(jnp.bfloat16) for i in (0, cols)]
    totals = [t.astype(jnp.bfloat16) for t in totals]
    for h in range(N_FAR):
        out_ref[h, :, :genes] = totals[0][h * cols : (h + 1) * cols]
        out_ref[h, :, genes : genes + LANES] = more[0]
        out_ref[h, :, genes + LANES : genes + 2 * LANES] = more[1]
        if len(totals) == 2:
            out_ref[h, :, genes + 2 * LANES :] = totals[1][h * cols : (h + 1) * cols]


def far_kernel(weight, total, place_ref, got_ref, coef_ref, *refs):
    cols, genes = coef_ref.shape
    refs, out_ref, obj_ref = refs[:-2], refs[-2], refs[-1]
    mirrored = len(refs) > 1
    picks = [r[...] for r in (refs[:2] if mirrored else refs)]
    band = picks[0].shape[0]
    got = got_ref[...]
    more = got[:, :, genes : genes + 2 * LANES].astype(jnp.float32)

    def row(i):
        at = i // cols * LANES
        return more[:, i % cols, at : at + LANES]

    vec, sc = join_rows(row, (genes + band) // LANES)
    totals, _, sc = merge(got, vec, sc, picks, weight, genes, band)
    tile, part = place_ref[0], place_ref[1]
    coef = coef_ref[...]
    rows_id = lax.broadcasted_iota(jnp.int32, coef.shape, 1) + tile * genes
    cols_id = lax.broadcasted_iota(jnp.int32, coef.shape, 0) + part * cols
    on_diag = rows_id == cols_id
    inverse = jnp.where(on_diag, 1.0 / jnp.where(on_diag, coef, 1.0), 0.0)
    stepped = coef - STEP * (totals[0] / total - inverse)
    limit = STEP * PENALTY
    shrunk = jnp.where(on_diag, stepped, stepped - jnp.clip(stepped, -limit, limit))
    out_ref[...] = shrunk
    if mirrored:
        order_ref, mirror_ref = refs[2:]
        stepped_m = mirror_ref[...] - STEP * (totals[1] / total)
        shrunk_m = stepped_m - jnp.clip(stepped_m, -limit, limit)
        shrunk_m = sum(dot(t, order_ref[...], (1, 0)) for t in split3(shrunk_m)[:2])
        top = shrunk[:, :band]
        out_ref[:, :band] = jnp.where(on_diag[:, :band], top, 0.5 * (top + shrunk_m))
    lane = lax.broadcasted_iota(jnp.int32, sc.shape, 1)
    factor = jnp.where(lane == 0, -1.0, jnp.where(lane == 1, PENALTY, jnp.where(lane == 2, 1.0 / (2.0 * total), 0.0)))
    obj_ref[...] = jnp.sum(sc * factor, axis=1, keepdims=True)


def kernel(fn, outs, in_specs=None):
    specs = {} if in_specs is None else {"in_specs": in_specs}
    return pl.pallas_call(
        fn, out_shape=outs, compiler_params=pltpu.CompilerParams(vmem_limit_bytes=48 * 2**20), **specs
    )


def spread(block, axes, n):
    shape = jax.ShapeDtypeStruct((n,) + block.shape[-2:], jnp.bfloat16)
    return lax.all_to_all(kernel(spread_kernel, shape)(block), axes, 0, 0)


def per_device(counts, coef):
    cells, genes = counts.shape
    cols = coef.shape[1]
    n_dp = N_FAR * N_NEAR
    band = cols * n_dp
    total = float(cells * n_dp)
    tile = lax.axis_index(TILE)
    near = lax.axis_index(NEAR)
    far = lax.axis_index(FAR)
    part = far * N_NEAR + near
    f32, bf16 = jnp.float32, jnp.bfloat16

    coef_t = coef.T
    w_far = spread(coef_t, FAR, N_FAR).reshape(N_FAR * cols, genes)

    rows_id = lax.broadcasted_iota(jnp.int32, (cols, genes), 1) + tile * genes
    cols_id = lax.broadcasted_iota(jnp.int32, (cols, genes), 0) + part * cols
    on_diag = rows_id == cols_id
    safe = jnp.where(on_diag, coef_t, 1.0)
    logsum = jnp.sum(jnp.where(on_diag, jnp.log(safe), 0.0))
    absolute = jnp.sum(jnp.where(on_diag, 0.0, jnp.abs(coef_t)))

    lib_rows = cells // 128
    lib = jnp.sum(counts, axis=1).astype(f32).reshape(lib_rows, 128)
    sums = jnp.pad(jnp.stack([logsum, absolute])[None], ((0, 7 - lib_rows % 8), (0, 126)))
    head = lax.psum(jnp.concatenate([lib, sums]), "y")
    w_far, head = lax.optimization_barrier((w_far, head))
    weights = spread(w_far, NEAR, N_NEAR).reshape(band, genes)
    head = lax.psum(lax.psum(head, "core"), "xl")
    library = head[:lib_rows].reshape(cells)

    scale = SCALE / (library + 1.0)
    expr = jnp.log(1.0 + counts.astype(f32) * scale[:, None]).astype(bf16)
    expr = lax.optimization_barrier(expr)
    sums_e = jnp.sum(expr.astype(f32), axis=0, keepdims=True)

    partial = dot(weights, expr, (1, 1))
    got = lax.all_to_all(partial.astype(bf16).reshape(N_TILE, band // N_TILE, cells), TILE, 0, 0)
    proj = spread(got, TILE, N_TILE).reshape(band, cells)

    head = head[lib_rows : lib_rows + 1]
    rows = N_FAR * cols

    def onehot(at, n):
        return (lax.broadcasted_iota(jnp.int32, (n, at.shape[0]), 0) == at[None, :]).astype(bf16)

    def tail(mirrored):
        wide = genes + (band if mirrored else 0)
        n_picks = 2 if mirrored else 1
        shape = jax.ShapeDtypeStruct((N_NEAR, rows, wide + LANES), bf16)
        got = kernel(functools.partial(pack_kernel, mirrored), shape)(proj, expr, sums_e, head)
        got = lax.all_to_all(got, NEAR, 0, 0)

        slot = jnp.arange(rows, dtype=jnp.int32)
        picks = [near * rows + slot, (slot // cols * N_NEAR + near) * cols + slot % cols]
        picks = [onehot(p, band) for p in picks[:n_picks]]
        shape = jax.ShapeDtypeStruct((N_FAR, cols, wide + 2 * LANES), bf16)
        got = kernel(functools.partial(near_kernel, float(cells), genes), shape)(got, *picks)
        got = lax.all_to_all(got, FAR, 0, 0)

        slot = jnp.arange(cols, dtype=jnp.int32)
        more = [onehot(p + slot, band) for p in (near * rows + far * cols, part * cols)[:n_picks]]
        if mirrored:
            nat = jnp.arange(band, dtype=jnp.int32)
            group = nat // cols
            more.append(onehot((group % N_NEAR * N_FAR + group // N_NEAR) * cols + nat % cols, band))
            more.append(dot(onehot(part * cols + slot, genes), weights, (0, 1)))
        place = jnp.stack([tile, part]).astype(jnp.int32)
        shapes = (jax.ShapeDtypeStruct((cols, genes), f32), jax.ShapeDtypeStruct((1, 1), f32))
        specs = [pl.BlockSpec(memory_space=pltpu.SMEM)] + [pl.BlockSpec(memory_space=pltpu.VMEM)] * (2 + len(more))
        return kernel(functools.partial(far_kernel, float(cells * N_NEAR), total), shapes, specs)(
            place, got, coef_t, *more
        )

    new_t, objective = lax.cond(tile == 0, lambda: tail(True), lambda: tail(False))
    return (new_t.T, objective[0, 0])


def solution(mesh):
    mesh = Mesh(mesh.devices.reshape(SIZES), AXES)
    return jax.shard_map(
        per_device,
        mesh=mesh,
        in_specs=(P((FAR,) + NEAR, TILE), P(TILE, (FAR,) + NEAR)),
        out_specs=(P(TILE, (FAR,) + NEAR), P()),
        check_vma=False,
    )
```

time: 160 us -> 155 us (0.969)
  the two profiles are of different devices: /device:TPU:6 before, /device:TPU:32 now
where the time goes in v5:
time: 155 us; the launch traced here: 154 us
  waiting for transfers between devices  59.4 us (38%)
  starting transfers between devices  37.8 us (24%)
  blocking collectives  36.6 us (24%)
  Pallas kernels  10 us (6%)
  other arithmetic  7.52 us (5%)
    all_to_all x3, starting transfers between devices, spread(): return lax.all_to_all(kernel(spread_kernel, shape)(block), axes, 0, 0)  24.1 us
    all_to_all x1, waiting for transfers between devices, tail(): got = lax.all_to_all(got, FAR, 0, 0)  23.1 us
    all_to_all x1, waiting for transfers between devices, tail(): got = lax.all_to_all(got, NEAR, 0, 0)  19 us
    all_to_all x1, blocking collectives, per_device(): lax.all_to_all(partial.astype(bf16).reshape(N_TILE, band // N_TILE, cells...  18 us
    all_to_all x3, waiting for transfers between devices, spread(): return lax.all_to_all(kernel(spread_kernel, shape)(block), axes, 0, 0)  17.4 us
    psum x1, blocking collectives, per_device(): head = lax.psum(jnp.concatenate([lib, sums]), 'y')  10.8 us
    psum x2, blocking collectives, per_device(): head = lax.psum(lax.psum(head, 'core'), 'xl')  7.91 us
    all_to_all x1, starting transfers between devices, tail(): got = lax.all_to_all(got, FAR, 0, 0)  7.61 us
  transfers between devices with their start and end apart: 5, of which 4 were waited for; matrix products, arithmetic and copies ran while one was open for 5% of the time, Pallas kernels for 0%

profile of v5, /device:TPU:32, one launch (start us, length us, event | category | flops | bytes accessed | tf_op | source)
XLA Modules:
  0.0 154.3 jit_solution(6499262675369454029)
XLA Ops:
  0.6 1.5 %shard_map.41 = bf16[8,16,1024]{2,1,0:T(8,128)(2,1)} custom-call(f32[16,1024]{1,0:T(8,128)} %bitcast.31), custom_call_target="tpu_custom_call" | custom-call | tf_op jit(solution)/shard_map/pallas_call | solution.py:170
  2.2 14.2 %all-to-all-start.4 = ((bf16[8,16,1024]{2,1,0:T(8,128)(2,1)}), bf16[8,16,1024]{2,1,0:T(8,128)(2,1)S(1)}, u32[]{:S(2)}, u32[]{:S(2)}) async-start(bf16[8,16,1024]{2,1,0:T(8,128)(2,1)} %shard_map.41), calls=%async_computation.4 | async-start | bytes 524288 | tf_op jit(solution)/shard_map/all_to_all | solution.py:170
  16.4 2.1 %reduce_sum.36 = s32[768]{0:T(1024)S(1)} reduce(s32[768,1024]{1,0:T(8,128)} %param.4, s32[]{:T(128)} %constant.115.clone.1), dimensions={1}, to_apply=%region_0.1 | reduce | flops 785664 | bytes 3148804 | tf_op jit(solution)/shard_map/reduce_sum | solution.py:196
  19.3 1.4 maximum_bitcast_fusion
  20.8 10.8 %psum.21 = f32[8,128]{1,0:T(8,128)S(1)} all-reduce(f32[8,128]{1,0:T(8,128)S(1)} %select_maximum_fusion), channel_id=1, replica_groups=mesh['zh'=8,'zl'=2,'xh'=2,'y'=4,'core'=2,'xl'=2] {'y'}, use_global_device_ids=true, to_apply=%region_3.4 | all-reduce | flops 1024 | bytes 8192 | tf_op jit(solution)/shard_map/psum | solution.py:198
  31.5 5.2 %all-to-all-done.4 = bf16[8,16,1024]{2,1,0:T(8,128)(2,1)S(1)} async-done(((bf16[8,16,1024]{2,1,0:T(8,128)(2,1)}), bf16[8,16,1024]{2,1,0:T(8,128)(2,1)S(1)}, u32[]{:S(2)}, u32[]{:S(2)}) %all-to-all-start.4) | async-done | bytes 262176 | tf_op jit(solution)/shard_map/all_to_all | solution.py:170
  36.8 1.0 shard_map.42
  37.8 6.3 %all-to-all-start.5 = ((bf16[4,128,1024]{2,1,0:T(8,128)(2,1)}), bf16[4,128,1024]{2,1,0:T(8,128)(2,1)S(1)}, u32[]{:S(2)}, u32[]{:S(2)}) async-start(bf16[4,128,1024]{2,1,0:T(8,128)(2,1)} %shard_map.42), calls=%async_computation.5 | async-start | bytes 2097152 | tf_op jit(solution)/shard_map/all_to_all | solution.py:170
  44.1 2.4 %psum.22 = f32[8,128]{1,0:T(8,128)S(1)} all-reduce(f32[8,128]{1,0:T(8,128)S(1)} %psum.21), channel_id=1, replica_groups=mesh['zh'=8,'zl'=2,'xh'=2,'y'=4,'core'=2,'xl'=2] {'core'}, use_global_device_ids=true, to_apply=%region_4.5 | all-reduce | flops 1024 | bytes 8192 | tf_op jit(solution)/shard_map/psum | solution.py:201
  46.5 5.5 %psum.23 = f32[8,128]{1,0:T(8,128)S(1)} all-reduce(f32[8,128]{1,0:T(8,128)S(1)} %psum.22), channel_id=1, replica_groups=mesh['zh'=8,'zl'=2,'xh'=2,'y'=4,'core'=2,'xl'=2] {'xl'}, use_global_device_ids=true, to_apply=%region_5.6 | all-reduce | flops 1024 | bytes 8192 | tf_op jit(solution)/shard_map/psum | solution.py:201
  52.0 2.5 %log_convert_fusion = bf16[768,1024]{1,0:T(8,128)(2,1)S(1)} fusion(s32[768,1024]{1,0:T(8,128)} %param.4, f32[768]{0:T(1024)S(1)} %divide_bitcast_fusion), kind=kLoop, calls=%fused_computation.60 | loop fusion | flops 3145728 | bytes 4721664 | tf_op jit(solution)/shard_map/convert_element_type | solution.py:205
  54.5 1.0 convolution_convert_fusion
  55.5 18.0 %all_to_all.36.block_ref = bf16[16,32,768]{2,1,0:T(8,128)(2,1)S(1)} all-to-all(bf16[16,32,768]{2,1,0:T(8,128)(2,1)S(1)} %bitcast.34), channel_id=1, replica_groups=mesh['zh'=8,'zl'=2,'xh'=2,'y'=4,'core'=2,'xl'=2] {'y','core','xl'}, dimensions={0} | all-to-all | bytes 1572864 | tf_op jit(solution)/shard_map/all_to_all | solution.py:210
  73.5 1.0 shard_map.43
  74.6 3.6 %all-to-all-start.7 = ((bf16[16,32,768]{2,1,0:T(8,128)(2,1)}), bf16[16,32,768]{2,1,0:T(8,128)(2,1)S(1)}, u32[]{:S(2)}, u32[]{:S(2)}) async-start(bf16[16,32,768]{2,1,0:T(8,128)(2,1)} %shard_map.43), calls=%async_computation.7 | async-start | bytes 1572864 | tf_op jit(solution)/shard_map/all_to_all | solution.py:170
  78.5 12.1 %all-to-all-done.7 = bf16[16,32,768]{2,1,0:T(8,128)(2,1)S(1)} async-done(((bf16[16,32,768]{2,1,0:T(8,128)(2,1)}), bf16[16,32,768]{2,1,0:T(8,128)(2,1)S(1)}, u32[]{:S(2)}, u32[]{:S(2)}) %all-to-all-start.7) | async-done | bytes 786464 | tf_op jit(solution)/shard_map/all_to_all | solution.py:170
  90.6 63.1 %conditional.1 = (f32[16,1024]{1,0:T(8,128)S(1)}, f32[]{:T(128)}) conditional(s32[]{:T(128)} %convert_element_type.46, (s32[]{:T(128)}, s32[]{:T(128)}, bf16[512,768]{1,0:T(8,128)(2,1)S(1)}, bf16[768,1024]{1,0:T(8,128)(2,1)S(1)}, f32[1,1024]{1,0:T(1,128)S(1)}, /*index=5*/f32[1,128]{1,0:T(1,128)S(1)}, s32[]{:T(128)}, s32[]{:T(128)}, ...), branch_computations={%region_7.8_spmd, %region_8.9_spmd} | conditional | flops 17649318 | bytes 8395232 | solution.py:247
  90.6 2.4 %branch_1_fun.3 = bf16[4,128,1664]{2,1,0:T(8,128)(2,1)} custom-call(bf16[512,768]{1,0:T(8,128)(2,1)S(1)} %get-tuple-element.56.proj_ref, bf16[768,1024]{1,0:T(8,128)(2,1)S(1)} %get-tuple-element.57.expr_ref, f32[1,1024]{1,0:T(1,128)S(1)} %get-tuple-element.58.sums_ref, f32[1,128]{1,0:T(1,128)S(1)} %get-tuple-element.59.head_ref), custom_call_target="tpu_custom_call" | custom-call | tf_op jit(solution)/shard_map/cond/branch_1_fun/pallas_call | solution.py:223
  93.0 6.1 %all-to-all-start.2 = ((bf16[4,128,1664]{2,1,0:T(8,128)(2,1)}), bf16[4,128,1664]{2,1,0:T(8,128)(2,1)S(1)}, u32[]{:S(2)}, u32[]{:S(2)}) async-start(bf16[4,128,1664]{2,1,0:T(8,128)(2,1)} %branch_1_fun.3), calls=%async_computation.2 | async-start | bytes 3407872 | tf_op jit(solution)/shard_map/cond/branch_1_fun/all_to_all | solution.py:224
  99.2 19.0 %all-to-all-done.2.got_ref = bf16[4,128,1664]{2,1,0:T(8,128)(2,1)S(1)} async-done(((bf16[4,128,1664]{2,1,0:T(8,128)(2,1)}), bf16[4,128,1664]{2,1,0:T(8,128)(2,1)S(1)}, u32[]{:S(2)}, u32[]{:S(2)}) %all-to-all-start.2) | async-done | bytes 1703968 | tf_op jit(solution)/shard_map/cond/branch_1_fun/all_to_all | solution.py:224
  118.3 2.0 %branch_1_fun.4 = bf16[8,16,1792]{2,1,0:T(8,128)(2,1)} custom-call(bf16[4,128,1664]{2,1,0:T(8,128)(2,1)S(1)} %all-to-all-done.2.got_ref, bf16[512,128]{1,0:T(8,128)(2,1)S(1)} %get-tuple-element.78.refs_0_, bf16[512,128]{1,0:T(8,128)(2,1)S(1)} %get-tuple-element.79.refs_1_), custom_call_target="tpu_custom_call" | custom-call | tf_op jit(solution)/shard_map/cond/branch_1_fun/pallas_call | solution.py:230
  120.3 7.6 %all-to-all-start.3 = ((bf16[8,16,1792]{2,1,0:T(8,128)(2,1)}), bf16[8,16,1792]{2,1,0:T(8,128)(2,1)S(1)}, u32[]{:S(2)}, u32[]{:S(2)}) async-start(bf16[8,16,1792]{2,1,0:T(8,128)(2,1)} %branch_1_fun.4), calls=%async_computation.3 | async-start | bytes 917504 | tf_op jit(solution)/shard_map/cond/branch_1_fun/all_to_all | solution.py:231
  128.6 23.1 %all-to-all-done.3.got_ref = bf16[8,16,1792]{2,1,0:T(8,128)(2,1)S(1)} async-done(((bf16[8,16,1792]{2,1,0:T(8,128)(2,1)}), bf16[8,16,1792]{2,1,0:T(8,128)(2,1)S(1)}, u32[]{:S(2)}, u32[]{:S(2)}) %all-to-all-start.3) | async-done | bytes 458784 | tf_op jit(solution)/shard_map/cond/branch_1_fun/all_to_all | solution.py:231
  151.7 2.0 %branch_1_fun.5 = (f32[16,1024]{1,0:T(8,128)S(1)}, f32[1,1]{1,0:T(1,128)}) custom-call(s32[2]{0:T(128)S(1)} %pad_add_fusion.1.place_ref, bf16[8,16,1792]{2,1,0:T(8,128)(2,1)S(1)} %all-to-all-done.3.got_ref, f32[16,1024]{1,0:T(8,128)S(1)} %get-tuple-element.61.coef_ref, bf16[512,16]{1,0:T(8,128)(2,1)S(1)} %get-tuple-element.80.refs_0_, ...), custom_call_target="tpu_custom_call" | custom-call | tf_op jit(solution)/shard_map/cond/branch_1_fun/pallas_call | solution.py:243
  (23 shorter events, 2.5 us)
Async XLA Ops:
  2.2 34.6 %all-to-all-start.4 = ((bf16[8,16,1024]{2,1,0:T(8,128)(2,1)}), bf16[8,16,1024]{2,1,0:T(8,128)(2,1)S(1)}, u32[]{:S(2)}, u32[]{:S(2)}) async-start(bf16[8,16,1024]{2,1,0:T(8,128)(2,1)} %shard_map.41), calls=%async_computation.4 | async-start | bytes 524288 | tf_op jit(solution)/shard_map/all_to_all | solution.py:170
  16.4 2.2 %copy-start = (f32[1024,16]{0,1:T(8,128)S(1)}, f32[1024,16]{0,1:T(8,128)}, u32[]{:S(2)}) copy-start(f32[1024,16]{0,1:T(8,128)} %param.5) | copy-start | bytes 196612
  37.8 16.7 %all-to-all-start.5 = ((bf16[4,128,1024]{2,1,0:T(8,128)(2,1)}), bf16[4,128,1024]{2,1,0:T(8,128)(2,1)S(1)}, u32[]{:S(2)}, u32[]{:S(2)}) async-start(bf16[4,128,1024]{2,1,0:T(8,128)(2,1)} %shard_map.42), calls=%async_computation.5 | async-start | bytes 2097152 | tf_op jit(solution)/shard_map/all_to_all | solution.py:170
  74.6 16.0 %all-to-all-start.7 = ((bf16[16,32,768]{2,1,0:T(8,128)(2,1)}), bf16[16,32,768]{2,1,0:T(8,128)(2,1)S(1)}, u32[]{:S(2)}, u32[]{:S(2)}) async-start(bf16[16,32,768]{2,1,0:T(8,128)(2,1)} %shard_map.43), calls=%async_computation.7 | async-start | bytes 1572864 | tf_op jit(solution)/shard_map/all_to_all | solution.py:170
  93.0 25.2 %all-to-all-start.2 = ((bf16[4,128,1664]{2,1,0:T(8,128)(2,1)}), bf16[4,128,1664]{2,1,0:T(8,128)(2,1)S(1)}, u32[]{:S(2)}, u32[]{:S(2)}) async-start(bf16[4,128,1664]{2,1,0:T(8,128)(2,1)} %branch_1_fun.3), calls=%async_computation.2 | async-start | bytes 3407872 | tf_op jit(solution)/shard_map/cond/branch_1_fun/all_to_all | solution.py:224
  120.3 31.4 %all-to-all-start.3 = ((bf16[8,16,1792]{2,1,0:T(8,128)(2,1)}), bf16[8,16,1792]{2,1,0:T(8,128)(2,1)S(1)}, u32[]{:S(2)}, u32[]{:S(2)}) async-start(bf16[8,16,1792]{2,1,0:T(8,128)(2,1)} %branch_1_fun.4), calls=%async_computation.3 | async-start | bytes 917504 | tf_op jit(solution)/shard_map/cond/branch_1_fun/all_to_all | solution.py:231
  153.6 0.6 copy-start.1

commit v6 on v5

--- a/solution.py
+++ b/solution.py
@@ -161,7 +161,7 @@
 def kernel(fn, outs, in_specs=None):
     specs = {} if in_specs is None else {"in_specs": in_specs}
     return pl.pallas_call(
-        fn, out_shape=outs, compiler_params=pltpu.CompilerParams(vmem_limit_bytes=48 * 2**20), **specs
+        fn, out_shape=outs, compiler_params=pltpu.CompilerParams(vmem_limit_bytes=24 * 2**20), **specs
     )
 
 
@@ -195,14 +195,14 @@
     lib_rows = cells // 128
     lib = jnp.sum(counts, axis=1).astype(f32).reshape(lib_rows, 128)
     sums = jnp.pad(jnp.stack([logsum, absolute])[None], ((0, 7 - lib_rows % 8), (0, 126)))
-    head = lax.psum(jnp.concatenate([lib, sums]), "y")
-    w_far, head = lax.optimization_barrier((w_far, head))
+    head = lax.psum(lax.psum(jnp.concatenate([lib, sums]), "y"), "core")
+    low, w_far, head = lax.optimization_barrier((counts.astype(bf16), w_far, head))
     weights = spread(w_far, NEAR, N_NEAR).reshape(band, genes)
-    head = lax.psum(lax.psum(head, "core"), "xl")
+    head = lax.psum(head, "xl")
     library = head[:lib_rows].reshape(cells)
 
     scale = SCALE / (library + 1.0)
-    expr = jnp.log(1.0 + counts.astype(f32) * scale[:, None]).astype(bf16)
+    expr = jnp.log(1.0 + low.astype(f32) * scale[:, None]).astype(bf16)
     expr = lax.optimization_barrier(expr)
     sums_e = jnp.sum(expr.astype(f32), axis=0, keepdims=True)
 

time: 155 us -> 160 us (1.032)
  waiting for transfers between devices: 59.4 us -> 54.4 us
  blocking collectives: 36.6 us -> 40.6 us
  starting transfers between devices: 37.8 us -> 41.4 us
  matrix products: 1.39 us -> 3.84 us
    psum x3, blocking collectives: 18.7 us -> 24.8 us  [the longest x2 13.2 us: per_device(): head = lax.psum(lax.psum(jnp.concatenate([lib, sums]), 'y'), 'core')]
    all_to_all x1, starting transfers between devices: 7.61 us -> 12.1 us  [tail(): got = lax.all_to_all(got, FAR, 0, 0)]
    all_to_all x3, waiting for transfers between devices: 17.4 us -> 14.3 us  [spread(): return lax.all_to_all(kernel(spread_kernel, shape)(block), axes, 0, 0)]
    dot_general x2, matrix products: 1.39 us -> 3.84 us  [dot(): lax.dot_general(a, b, ((dims[:1], dims[1:]), ((), ())), preferred_element...]
    all_to_all x1, blocking collectives: 18 us -> 15.7 us  [per_device(): lax.all_to_all(partial.astype(bf16).reshape(N_TILE, band // N_TILE, cells...]
    all_to_all x1, waiting for transfers between devices: 23.1 us -> 21.1 us  [tail(): got = lax.all_to_all(got, FAR, 0, 0)]
    convert_element_type x1, other arithmetic: 2.51 us -> 0.64 us  [per_device(): expr = jnp.log(1.0 + low.astype(f32) * scale[:, None]).astype(bf16)]
  transfers between devices with their start and end apart: 5 -> 5, of which waited for: 4 -> 5; matrix products, arithmetic and copies ran while one was open for 5% -> 6% of each run, Pallas kernels for 0% -> 0%
where the time goes in v6:
time: 160 us; the launch traced here: 159 us
  waiting for transfers between devices  54.4 us (34%)
  starting transfers between devices  41.4 us (26%)
  blocking collectives  40.6 us (25%)
  Pallas kernels  10.3 us (6%)
  other arithmetic  7.61 us (5%)
  matrix products  3.84 us (2%)
    all_to_all x3, starting transfers between devices, spread(): return lax.all_to_all(kernel(spread_kernel, shape)(block), axes, 0, 0)  24.2 us
    all_to_all x1, waiting for transfers between devices, tail(): got = lax.all_to_all(got, FAR, 0, 0)  21.1 us
    all_to_all x1, waiting for transfers between devices, tail(): got = lax.all_to_all(got, NEAR, 0, 0)  19 us
    all_to_all x1, blocking collectives, per_device(): lax.all_to_all(partial.astype(bf16).reshape(N_TILE, band // N_TILE, cells...  15.7 us
    all_to_all x3, waiting for transfers between devices, spread(): return lax.all_to_all(kernel(spread_kernel, shape)(block), axes, 0, 0)  14.3 us
    psum x2, blocking collectives, per_device(): head = lax.psum(lax.psum(jnp.concatenate([lib, sums]), 'y'), 'core')  13.2 us
    all_to_all x1, starting transfers between devices, tail(): got = lax.all_to_all(got, FAR, 0, 0)  12.1 us
    psum x1, blocking collectives, per_device(): head = lax.psum(head, 'xl')  11.6 us
  transfers between devices with their start and end apart: 5, of which 5 were waited for; matrix products, arithmetic and copies ran while one was open for 6% of the time, Pallas kernels for 0%

profile of v6, /device:TPU:32, one launch (start us, length us, event | category | flops | bytes accessed | tf_op | source)
XLA Modules:
  0.0 158.9 jit_solution(4186844293300973676)
XLA Ops:
  0.6 1.6 shard_map.41
  2.2 14.2 %all-to-all-start.4 = ((bf16[8,16,1024]{2,1,0:T(8,128)(2,1)}), bf16[8,16,1024]{2,1,0:T(8,128)(2,1)S(1)}, u32[]{:S(2)}, u32[]{:S(2)}) async-start(bf16[8,16,1024]{2,1,0:T(8,128)(2,1)} %shard_map.41), calls=%async_computation.4 | async-start | bytes 524288 | tf_op jit(solution)/shard_map/all_to_all | solution.py:170
  16.4 1.5 fusion.32
  17.9 1.4 maximum_bitcast_fusion
  19.3 3.4 %fusion.34 = (s32[768]{0:T(1024)S(1)}, bf16[768,1024]{1,0:T(8,128)(2,1)S(1)}) fusion(s32[768,1024]{1,0:T(8,128)} %param.4), kind=kLoop, calls=%fused_computation.75 | loop fusion | flops 1572096 | bytes 4721664 | tf_op jit(solution)/shard_map/reduce_sum | solution.py:196
  22.7 10.8 %psum.21 = f32[8,128]{1,0:T(8,128)S(1)} all-reduce(f32[8,128]{1,0:T(8,128)S(1)} %select_maximum_fusion), channel_id=1, replica_groups=mesh['zh'=8,'zl'=2,'xh'=2,'y'=4,'core'=2,'xl'=2] {'y'}, use_global_device_ids=true, to_apply=%region_3.4 | all-reduce | flops 1024 | bytes 8192 | tf_op jit(solution)/shard_map/psum | solution.py:198
  33.5 2.5 %psum.22 = f32[8,128]{1,0:T(8,128)S(1)} all-reduce(f32[8,128]{1,0:T(8,128)S(1)} %psum.21), channel_id=1, replica_groups=mesh['zh'=8,'zl'=2,'xh'=2,'y'=4,'core'=2,'xl'=2] {'core'}, use_global_device_ids=true, to_apply=%region_4.5 | all-reduce | flops 1024 | bytes 8192 | tf_op jit(solution)/shard_map/psum | solution.py:198
  36.8 1.0 shard_map.42
  37.8 6.3 %all-to-all-start.5 = ((bf16[4,128,1024]{2,1,0:T(8,128)(2,1)}), bf16[4,128,1024]{2,1,0:T(8,128)(2,1)}, u32[]{:S(2)}, u32[]{:S(2)}) async-start(bf16[4,128,1024]{2,1,0:T(8,128)(2,1)} %shard_map.42), calls=%async_computation.5 | async-start | bytes 2097152 | tf_op jit(solution)/shard_map/all_to_all | solution.py:170
  44.1 11.6 %psum.23 = f32[8,128]{1,0:T(8,128)S(1)} all-reduce(f32[8,128]{1,0:T(8,128)S(1)} %psum.22), channel_id=1, replica_groups=mesh['zh'=8,'zl'=2,'xh'=2,'y'=4,'core'=2,'xl'=2] {'xl'}, use_global_device_ids=true, to_apply=%region_5.6 | all-reduce | flops 1024 | bytes 8192 | tf_op jit(solution)/shard_map/psum | solution.py:201
  56.4 1.4 all-to-all-done.5
  57.8 2.2 %convolution_convert_fusion = bf16[512,768]{1,0:T(8,128)(2,1)S(1)} fusion(bf16[512,1024]{1,0:T(8,128)(2,1)} %bitcast.12, bf16[768,1024]{1,0:T(8,128)(2,1)S(1)} %log_convert_fusion), kind=kOutput, calls=%fused_computation.61 | convolution fusion | flops 805699584 | bytes 3407872 | tf_op jit(solution)/shard_map/dot_general | solution.py:24
  60.0 15.7 %all_to_all.36.block_ref = bf16[16,32,768]{2,1,0:T(8,128)(2,1)S(1)} all-to-all(bf16[16,32,768]{2,1,0:T(8,128)(2,1)S(1)} %bitcast.32), channel_id=1, replica_groups=mesh['zh'=8,'zl'=2,'xh'=2,'y'=4,'core'=2,'xl'=2] {'y','core','xl'}, dimensions={0} | all-to-all | bytes 1572864 | tf_op jit(solution)/shard_map/all_to_all | solution.py:210
  76.8 3.7 %all-to-all-start.7 = ((bf16[16,32,768]{2,1,0:T(8,128)(2,1)}), bf16[16,32,768]{2,1,0:T(8,128)(2,1)S(1)}, u32[]{:S(2)}, u32[]{:S(2)}) async-start(bf16[16,32,768]{2,1,0:T(8,128)(2,1)} %shard_map.43), calls=%async_computation.7 | async-start | bytes 1572864 | tf_op jit(solution)/shard_map/all_to_all | solution.py:170
  80.8 12.1 %all-to-all-done.7 = bf16[16,32,768]{2,1,0:T(8,128)(2,1)S(1)} async-done(((bf16[16,32,768]{2,1,0:T(8,128)(2,1)}), bf16[16,32,768]{2,1,0:T(8,128)(2,1)S(1)}, u32[]{:S(2)}, u32[]{:S(2)}) %all-to-all-start.7) | async-done | bytes 786464 | tf_op jit(solution)/shard_map/all_to_all | solution.py:170
  92.9 65.9 %conditional.1 = (f32[16,1024]{1,0:T(8,128)}, f32[]{:T(128)}) conditional(s32[]{:T(128)} %convert_element_type.49, (s32[]{:T(128)}, s32[]{:T(128)}, bf16[512,768]{1,0:T(8,128)(2,1)S(1)}, bf16[768,1024]{1,0:T(8,128)(2,1)S(1)}, f32[1,1024]{1,0:T(1,128)S(1)}, /*index=5*/f32[1,128]{1,0:T(1,128)S(1)}, s32[]{:T(128)}, s32[]{:T(128)}, ...), branch_computations={%region_7.8_spmd, %region_8.9_spmd} | conditional | flops 17649318 | bytes 8919576 | solution.py:247
  92.9 2.4 %branch_1_fun.3 = bf16[4,128,1664]{2,1,0:T(8,128)(2,1)} custom-call(bf16[512,768]{1,0:T(8,128)(2,1)S(1)} %get-tuple-element.56.proj_ref, bf16[768,1024]{1,0:T(8,128)(2,1)S(1)} %get-tuple-element.57.expr_ref, f32[1,1024]{1,0:T(1,128)S(1)} %get-tuple-element.58.sums_ref, f32[1,128]{1,0:T(1,128)S(1)} %get-tuple-element.59.head_ref), custom_call_target="tpu_custom_call" | custom-call | tf_op jit(solution)/shard_map/cond/branch_1_fun/pallas_call | solution.py:223
  95.4 5.0 %all-to-all-start.2 = ((bf16[4,128,1664]{2,1,0:T(8,128)(2,1)}), bf16[4,128,1664]{2,1,0:T(8,128)(2,1)S(1)}, u32[]{:S(2)}, u32[]{:S(2)}) async-start(bf16[4,128,1664]{2,1,0:T(8,128)(2,1)} %branch_1_fun.3), calls=%async_computation.2 | async-start | bytes 3407872 | tf_op jit(solution)/shard_map/cond/branch_1_fun/all_to_all | solution.py:224
  100.5 19.0 %all-to-all-done.2.got_ref = bf16[4,128,1664]{2,1,0:T(8,128)(2,1)S(1)} async-done(((bf16[4,128,1664]{2,1,0:T(8,128)(2,1)}), bf16[4,128,1664]{2,1,0:T(8,128)(2,1)S(1)}, u32[]{:S(2)}, u32[]{:S(2)}) %all-to-all-start.2) | async-done | bytes 1703968 | tf_op jit(solution)/shard_map/cond/branch_1_fun/all_to_all | solution.py:224
  119.5 2.0 %branch_1_fun.4 = bf16[8,16,1792]{2,1,0:T(8,128)(2,1)} custom-call(bf16[4,128,1664]{2,1,0:T(8,128)(2,1)S(1)} %all-to-all-done.2.got_ref, bf16[512,128]{1,0:T(8,128)(2,1)S(1)} %get-tuple-element.80.refs_0_, bf16[512,128]{1,0:T(8,128)(2,1)S(1)} %get-tuple-element.81.refs_1_), custom_call_target="tpu_custom_call" | custom-call | tf_op jit(solution)/shard_map/cond/branch_1_fun/pallas_call | solution.py:230
  121.6 12.1 %all-to-all-start.3 = ((bf16[8,16,1792]{2,1,0:T(8,128)(2,1)}), bf16[8,16,1792]{2,1,0:T(8,128)(2,1)S(1)}, u32[]{:S(2)}, u32[]{:S(2)}) async-start(bf16[8,16,1792]{2,1,0:T(8,128)(2,1)} %branch_1_fun.4), calls=%async_computation.3 | async-start | bytes 917504 | tf_op jit(solution)/shard_map/cond/branch_1_fun/all_to_all | solution.py:231
  134.0 1.6 %fusion.4.refs_3_ = f32[16,512]{1,0:T(8,128)S(1)} fusion(bf16[512,1024]{1,0:T(8,128)(2,1)} %get-tuple-element.63, s32[16]{0:T(128)S(1)} %iota_add_fusion.2), kind=kOutput, calls=%fused_computation.11 | convolution fusion | flops 16809984 | bytes 1081408 | tf_op jit(solution)/shard_map/cond/branch_1_fun/dot_general | solution.py:24
  135.6 21.1 %all-to-all-done.3.got_ref = bf16[8,16,1792]{2,1,0:T(8,128)(2,1)S(1)} async-done(((bf16[8,16,1792]{2,1,0:T(8,128)(2,1)}), bf16[8,16,1792]{2,1,0:T(8,128)(2,1)S(1)}, u32[]{:S(2)}, u32[]{:S(2)}) %all-to-all-start.3) | async-done | bytes 458784 | tf_op jit(solution)/shard_map/cond/branch_1_fun/all_to_all | solution.py:231
  156.7 2.2 %branch_1_fun.5 = (f32[16,1024]{1,0:T(8,128)}, f32[1,1]{1,0:T(1,128)}) custom-call(s32[2]{0:T(128)S(1)} %pad_add_fusion.1.place_ref, bf16[8,16,1792]{2,1,0:T(8,128)(2,1)S(1)} %all-to-all-done.3.got_ref, f32[16,1024]{1,0:T(8,128)S(1)} %copy-done.2, bf16[512,16]{1,0:T(8,128)(2,1)S(1)} %get-tuple-element.82.refs_0_, ...), custom_call_target="tpu_custom_call" | custom-call | tf_op jit(solution)/shard_map/cond/branch_1_fun/pallas_call | solution.py:243
  (25 shorter events, 3.2 us)
Async XLA Ops:
  2.2 34.6 %all-to-all-start.4 = ((bf16[8,16,1024]{2,1,0:T(8,128)(2,1)}), bf16[8,16,1024]{2,1,0:T(8,128)(2,1)S(1)}, u32[]{:S(2)}, u32[]{:S(2)}) async-start(bf16[8,16,1024]{2,1,0:T(8,128)(2,1)} %shard_map.41), calls=%async_computation.4 | async-start | bytes 524288 | tf_op jit(solution)/shard_map/all_to_all | solution.py:170
  37.8 20.0 %all-to-all-start.5 = ((bf16[4,128,1024]{2,1,0:T(8,128)(2,1)}), bf16[4,128,1024]{2,1,0:T(8,128)(2,1)}, u32[]{:S(2)}, u32[]{:S(2)}) async-start(bf16[4,128,1024]{2,1,0:T(8,128)(2,1)} %shard_map.42), calls=%async_computation.5 | async-start | bytes 2097152 | tf_op jit(solution)/shard_map/all_to_all | solution.py:170
  76.8 16.2 %copy-start = (f32[1024,16]{0,1:T(8,128)S(1)}, f32[1024,16]{0,1:T(8,128)}, u32[]{:S(2)}) copy-start(f32[1024,16]{0,1:T(8,128)} %param.5) | copy-start | bytes 196612
  76.8 16.2 %all-to-all-start.7 = ((bf16[16,32,768]{2,1,0:T(8,128)(2,1)}), bf16[16,32,768]{2,1,0:T(8,128)(2,1)S(1)}, u32[]{:S(2)}, u32[]{:S(2)}) async-start(bf16[16,32,768]{2,1,0:T(8,128)(2,1)} %shard_map.43), calls=%async_computation.7 | async-start | bytes 1572864 | tf_op jit(solution)/shard_map/all_to_all | solution.py:170
  92.9 2.5 %copy-start.1 = (f32[16,1024]{1,0:T(8,128)}, f32[16,1024]{1,0:T(8,128)S(1)}, u32[]{:S(2)}) copy-start(f32[16,1024]{1,0:T(8,128)S(1)} %get-tuple-element.61.coef_ref) | copy-start | bytes 196612 | tf_op jit(solution)/shard_map/cond
  95.4 24.1 %all-to-all-start.2 = ((bf16[4,128,1664]{2,1,0:T(8,128)(2,1)}), bf16[4,128,1664]{2,1,0:T(8,128)(2,1)S(1)}, u32[]{:S(2)}, u32[]{:S(2)}) async-start(bf16[4,128,1664]{2,1,0:T(8,128)(2,1)} %branch_1_fun.3), calls=%async_computation.2 | async-start | bytes 3407872 | tf_op jit(solution)/shard_map/cond/branch_1_fun/all_to_all | solution.py:224
  121.6 35.1 %copy-start.2 = (f32[16,1024]{1,0:T(8,128)S(1)}, f32[16,1024]{1,0:T(8,128)}, u32[]{:S(2)}) copy-start(f32[16,1024]{1,0:T(8,128)} %copy-done.1) | copy-start | bytes 196612 | tf_op jit(solution)/shard_map/cond
  121.6 35.1 %all-to-all-start.3 = ((bf16[8,16,1792]{2,1,0:T(8,128)(2,1)}), bf16[8,16,1792]{2,1,0:T(8,128)(2,1)S(1)}, u32[]{:S(2)}, u32[]{:S(2)}) async-start(bf16[8,16,1792]{2,1,0:T(8,128)(2,1)} %branch_1_fun.4), calls=%async_computation.3 | async-start | bytes 917504 | tf_op jit(solution)/shard_map/cond/branch_1_fun/all_to_all | solution.py:231

commit v7 on v5

--- a/solution.py
+++ b/solution.py
@@ -40,6 +40,39 @@
 def join_rows(row, n):
     vec = jnp.concatenate([row(n + i) + row(i) for i in range(n)], axis=1)
     return vec, row(2 * n + 2) + row(2 * n + 1) + row(2 * n)
+
+
+def diagonal(shape, place_ref):
+    rows_id = lax.broadcasted_iota(jnp.int32, shape, 1) + place_ref[0] * shape[1]
+    cols_id = lax.broadcasted_iota(jnp.int32, shape, 0) + place_ref[1] * shape[0]
+    return rows_id == cols_id
+
+
+def head_kernel(place_ref, counts_ref, coef_ref, head_ref, low_ref):
+    step = pl.program_id(0)
+    per_step = counts_ref.shape[0] // LANES
+
+    @pl.when(step == 0)
+    def _():
+        coef = coef_ref[...]
+        on_diag = diagonal(coef.shape, place_ref)
+        logsum = jnp.sum(jnp.where(on_diag, jnp.log(jnp.where(on_diag, coef, 1.0)), 0.0))
+        absolute = jnp.sum(jnp.where(on_diag, 0.0, jnp.abs(coef)))
+        at = lax.broadcasted_iota(jnp.int32, head_ref.shape, 0)
+        lane = lax.broadcasted_iota(jnp.int32, head_ref.shape, 1)
+        row = jnp.where(lane == 0, logsum, jnp.where(lane == 1, absolute, 0.0))
+        head_ref[...] = jnp.where(at == pl.num_programs(0) * per_step, row, 0.0)
+
+    for i in range(per_step):
+        rows = slice(i * LANES, (i + 1) * LANES)
+        low = counts_ref[rows].astype(jnp.float32).astype(jnp.bfloat16)
+        low_ref[rows] = low
+        sums = dot(jnp.ones((8, low.shape[1]), jnp.bfloat16), low, (1, 1))
+        head_ref[pl.ds(step * per_step + i, 1), :] = sums[:1]
+
+
+def project_kernel(weights_ref, expr_ref, out_ref):
+    out_ref[...] = dot(weights_ref[...], expr_ref[...], (1, 1)).astype(jnp.bfloat16)
 
 
 def spread_kernel(block_ref, out_ref):
@@ -87,9 +120,9 @@
     dm, dw = diff[:, :genes], diff[:, genes:]
 
     def total(part, left, right, pick):
-        left = sum(dot(t, pick, (1, 0)) for t in split3(left))
+        left = weight * sum(dot(pick, t, (1, 1)) for t in split3(left))
         out = sum(part[i].astype(jnp.float32) for i in range(n))
-        return out + weight * dot(left, right, (0, 0), precision=lax.Precision.HIGHEST)
+        return out + sum(left[:, i : i + 1] * right[i : i + 1] for i in range(n))
 
     totals = [total(got[:, :, :genes], dw, dm, picks[0])]
     if len(picks) == 2:
@@ -103,7 +136,7 @@
 def near_kernel(weight, genes, got_ref, *refs):
     n, rows, wide = got_ref.shape
     picks, out_ref = [r[...] for r in refs[:-1]], refs[-1]
-    band = picks[0].shape[0]
+    band = picks[0].shape[1]
     cols = rows // N_FAR
     got = got_ref[...]
     more = [got[i, :32, genes : genes + LANES].astype(jnp.float32) for i in range(n)]
@@ -126,7 +159,7 @@
     refs, out_ref, obj_ref = refs[:-2], refs[-2], refs[-1]
     mirrored = len(refs) > 1
     picks = [r[...] for r in (refs[:2] if mirrored else refs)]
-    band = picks[0].shape[0]
+    band = picks[0].shape[1]
     got = got_ref[...]
     more = got[:, :, genes : genes + 2 * LANES].astype(jnp.float32)
 
@@ -136,11 +169,8 @@
 
     vec, sc = join_rows(row, (genes + band) // LANES)
     totals, _, sc = merge(got, vec, sc, picks, weight, genes, band)
-    tile, part = place_ref[0], place_ref[1]
     coef = coef_ref[...]
-    rows_id = lax.broadcasted_iota(jnp.int32, coef.shape, 1) + tile * genes
-    cols_id = lax.broadcasted_iota(jnp.int32, coef.shape, 0) + part * cols
-    on_diag = rows_id == cols_id
+    on_diag = diagonal(coef.shape, place_ref)
     inverse = jnp.where(on_diag, 1.0 / jnp.where(on_diag, coef, 1.0), 0.0)
     stepped = coef - STEP * (totals[0] / total - inverse)
     limit = STEP * PENALTY
@@ -150,7 +180,7 @@
         order_ref, mirror_ref = refs[2:]
         stepped_m = mirror_ref[...] - STEP * (totals[1] / total)
         shrunk_m = stepped_m - jnp.clip(stepped_m, -limit, limit)
-        shrunk_m = sum(dot(t, order_ref[...], (1, 0)) for t in split3(shrunk_m)[:2])
+        shrunk_m = sum(dot(t, order_ref[...], (1, 1)) for t in split3(shrunk_m)[:2])
         top = shrunk[:, :band]
         out_ref[:, :band] = jnp.where(on_diag[:, :band], top, 0.5 * (top + shrunk_m))
     lane = lax.broadcasted_iota(jnp.int32, sc.shape, 1)
@@ -185,36 +215,50 @@
     coef_t = coef.T
     w_far = spread(coef_t, FAR, N_FAR).reshape(N_FAR * cols, genes)
 
-    rows_id = lax.broadcasted_iota(jnp.int32, (cols, genes), 1) + tile * genes
-    cols_id = lax.broadcasted_iota(jnp.int32, (cols, genes), 0) + part * cols
-    on_diag = rows_id == cols_id
-    safe = jnp.where(on_diag, coef_t, 1.0)
-    logsum = jnp.sum(jnp.where(on_diag, jnp.log(safe), 0.0))
-    absolute = jnp.sum(jnp.where(on_diag, 0.0, jnp.abs(coef_t)))
-
-    lib_rows = cells // 128
-    lib = jnp.sum(counts, axis=1).astype(f32).reshape(lib_rows, 128)
-    sums = jnp.pad(jnp.stack([logsum, absolute])[None], ((0, 7 - lib_rows % 8), (0, 126)))
-    head = lax.psum(jnp.concatenate([lib, sums]), "y")
+    place = jnp.stack([tile, part]).astype(jnp.int32)
+    lib_rows = cells // LANES
+    head, low = pl.pallas_call(
+        head_kernel,
+        grid=(2,),
+        in_specs=[
+            pl.BlockSpec(memory_space=pltpu.SMEM),
+            pl.BlockSpec((cells // 2, genes), lambda i: (i, 0)),
+            pl.BlockSpec((cols, genes), lambda i: (0, 0)),
+        ],
+        out_specs=[
+            pl.BlockSpec((lib_rows // 8 * 8 + 8, LANES), lambda i: (0, 0)),
+            pl.BlockSpec((cells // 2, genes), lambda i: (i, 0)),
+        ],
+        out_shape=[
+            jax.ShapeDtypeStruct((lib_rows // 8 * 8 + 8, LANES), f32),
+            jax.ShapeDtypeStruct((cells, genes), bf16),
+        ],
+        compiler_params=pltpu.CompilerParams(vmem_limit_bytes=60 * 2**20),
+    )(place, counts, coef_t)
+
+    head = lax.psum(head, "core")
+    head = lax.psum(head, "xl")
     w_far, head = lax.optimization_barrier((w_far, head))
     weights = spread(w_far, NEAR, N_NEAR).reshape(band, genes)
-    head = lax.psum(lax.psum(head, "core"), "xl")
+    head = lax.psum(head, "y")
     library = head[:lib_rows].reshape(cells)
 
     scale = SCALE / (library + 1.0)
-    expr = jnp.log(1.0 + counts.astype(f32) * scale[:, None]).astype(bf16)
+    expr = jnp.log(1.0 + low.astype(f32) * scale[:, None]).astype(bf16)
     expr = lax.optimization_barrier(expr)
     sums_e = jnp.sum(expr.astype(f32), axis=0, keepdims=True)
 
-    partial = dot(weights, expr, (1, 1))
-    got = lax.all_to_all(partial.astype(bf16).reshape(N_TILE, band // N_TILE, cells), TILE, 0, 0)
+    partial = kernel(project_kernel, jax.ShapeDtypeStruct((band, cells), bf16))(weights, expr)
+    got = lax.all_to_all(partial.reshape(N_TILE, band // N_TILE, cells), TILE, 0, 0)
     proj = spread(got, TILE, N_TILE).reshape(band, cells)
 
     head = head[lib_rows : lib_rows + 1]
     rows = N_FAR * cols
 
     def onehot(at, n):
-        return (lax.broadcasted_iota(jnp.int32, (n, at.shape[0]), 0) == at[None, :]).astype(bf16)
+        return (lax.broadcasted_iota(jnp.int32, (at.shape[0], n), 1) == at[:, None]).astype(bf16)
+
+    coef_m = dot(onehot(part * cols + jnp.arange(cols, dtype=jnp.int32), genes), weights, (1, 1))
 
     def tail(mirrored):
         wide = genes + (band if mirrored else 0)
@@ -236,8 +280,7 @@
             nat = jnp.arange(band, dtype=jnp.int32)
             group = nat // cols
             more.append(onehot((group % N_NEAR * N_FAR + group // N_NEAR) * cols + nat % cols, band))
-            more.append(dot(onehot(part * cols + slot, genes), weights, (0, 1)))
-        place = jnp.stack([tile, part]).astype(jnp.int32)
+            more.append(coef_m)
         shapes = (jax.ShapeDtypeStruct((cols, genes), f32), jax.ShapeDtypeStruct((1, 1), f32))
         specs = [pl.BlockSpec(memory_space=pltpu.SMEM)] + [pl.BlockSpec(memory_space=pltpu.VMEM)] * (2 + len(more))
         return kernel(functools.partial(far_kernel, float(cells * N_NEAR), total), shapes, specs)(

time: 155 us -> 152 us (0.981)
  other arithmetic: 7.52 us -> 2.76 us
  waiting for transfers between devices: 59.4 us -> 63.8 us
  Pallas kernels: 10 us -> 13.3 us
  blocking collectives: 36.6 us -> 33.8 us
  starting transfers between devices: 37.8 us -> 35.4 us
    all_to_all x3, waiting for transfers between devices: 17.4 us -> 21.6 us  [spread(): return lax.all_to_all(kernel(spread_kernel, shape)(block), axes, 0, 0)]
    pallas_call x0 -> x2, Pallas kernels: none -> 3.98 us  [the longest x1 2.97 us: per_device(): pl.pallas_call(head_kernel, grid=(2,), in_specs=[pl.BlockSpec(memory_spac...]
    reduce_sum x2 -> x0, other arithmetic: 2.91 us -> none  [the longest x1 2.14 us: per_device(): lib = jnp.sum(counts, axis=1).astype(f32).reshape(lib_rows, 128)]
    all_to_all x1, blocking collectives: 18 us -> 15.6 us  [per_device(): lax.all_to_all(partial.reshape(N_TILE, band // N_TILE, cells), TILE, 0, 0)]
    all_to_all x1, starting transfers between devices: 7.61 us -> 5.45 us  [tail(): got = lax.all_to_all(got, FAR, 0, 0)]
  transfers between devices with their start and end apart: 5 -> 5, of which waited for: 4 -> 4; matrix products, arithmetic and copies ran while one was open for 5% -> 2% of each run, Pallas kernels for 0% -> 2%
where the time goes in v7:
time: 152 us; the launch traced here: 151 us
  waiting for transfers between devices  63.8 us (42%)
  starting transfers between devices  35.4 us (23%)
  blocking collectives  33.8 us (22%)
  Pallas kernels  13.3 us (9%)
  other arithmetic  2.76 us (2%)
    all_to_all x3, starting transfers between devices, spread(): return lax.all_to_all(kernel(spread_kernel, shape)(block), axes, 0, 0)  24.1 us
    all_to_all x1, waiting for transfers between devices, tail(): got = lax.all_to_all(got, FAR, 0, 0)  23.2 us
    all_to_all x3, waiting for transfers between devices, spread(): return lax.all_to_all(kernel(spread_kernel, shape)(block), axes, 0, 0)  21.6 us
    all_to_all x1, waiting for transfers between devices, tail(): got = lax.all_to_all(got, NEAR, 0, 0)  19 us
    all_to_all x1, blocking collectives, per_device(): lax.all_to_all(partial.reshape(N_TILE, band // N_TILE, cells), TILE, 0, 0)  15.6 us
    psum x1, blocking collectives, per_device(): head = lax.psum(head, 'y')  10.7 us
    all_to_all x1, starting transfers between devices, tail(): got = lax.all_to_all(got, NEAR, 0, 0)  5.89 us
    all_to_all x1, starting transfers between devices, tail(): got = lax.all_to_all(got, FAR, 0, 0)  5.45 us
  transfers between devices with their start and end apart: 5, of which 4 were waited for; matrix products, arithmetic and copies ran while one was open for 2% of the time, Pallas kernels for 2%

profile of v7, /device:TPU:32, one launch (start us, length us, event | category | flops | bytes accessed | tf_op | source)
XLA Modules:
  0.0 150.8 jit_solution(11759528553238558189)
XLA Ops:
  0.6 1.6 %shard_map.41 = bf16[8,16,1024]{2,1,0:T(8,128)(2,1)} custom-call(f32[16,1024]{1,0:T(8,128)} %bitcast.20), custom_call_target="tpu_custom_call" | custom-call | tf_op jit(solution)/shard_map/pallas_call | solution.py:200
  2.2 14.2 %all-to-all-start.4 = ((bf16[8,16,1024]{2,1,0:T(8,128)(2,1)}), bf16[8,16,1024]{2,1,0:T(8,128)(2,1)S(1)}, u32[]{:S(2)}, u32[]{:S(2)}) async-start(bf16[8,16,1024]{2,1,0:T(8,128)(2,1)} %shard_map.41), calls=%async_computation.4 | async-start | bytes 524288 | tf_op jit(solution)/shard_map/all_to_all | solution.py:200
  16.5 3.0 %shard_map.42 = (f32[8,128]{1,0:T(8,128)}, bf16[768,1024]{1,0:T(8,128)(2,1)}) custom-call(s32[2]{0:T(128)S(1)} %pad_add_fusion.place_ref, s32[768,1024]{1,0:T(8,128)} %counts_ref.1, f32[16,1024]{1,0:T(8,128)} %bitcast.21), custom_call_target="tpu_custom_call" | custom-call | tf_op jit(solution)/shard_map/pallas_call | solution.py:220
  19.4 2.6 %psum.21 = f32[8,128]{1,0:T(8,128)S(1)} all-reduce(f32[8,128]{1,0:T(8,128)} %get-tuple-element.71), channel_id=1, replica_groups=mesh['zh'=8,'zl'=2,'xh'=2,'y'=4,'core'=2,'xl'=2] {'core'}, use_global_device_ids=true, to_apply=%region_0.0 | all-reduce | flops 1024 | bytes 8192 | tf_op jit(solution)/shard_map/psum | solution.py:239
  22.0 4.9 %psum.22 = f32[8,128]{1,0:T(8,128)S(1)} all-reduce(f32[8,128]{1,0:T(8,128)S(1)} %psum.21), channel_id=1, replica_groups=mesh['zh'=8,'zl'=2,'xh'=2,'y'=4,'core'=2,'xl'=2] {'xl'}, use_global_device_ids=true, to_apply=%region_1.0 | all-reduce | flops 1024 | bytes 8192 | tf_op jit(solution)/shard_map/psum | solution.py:240
  26.9 9.8 %all-to-all-done.4 = bf16[8,16,1024]{2,1,0:T(8,128)(2,1)S(1)} async-done(((bf16[8,16,1024]{2,1,0:T(8,128)(2,1)}), bf16[8,16,1024]{2,1,0:T(8,128)(2,1)S(1)}, u32[]{:S(2)}, u32[]{:S(2)}) %all-to-all-start.4) | async-done | bytes 262176 | tf_op jit(solution)/shard_map/all_to_all | solution.py:200
  36.8 1.1 shard_map.43
  37.8 6.3 %all-to-all-start.5 = ((bf16[4,128,1024]{2,1,0:T(8,128)(2,1)}), bf16[4,128,1024]{2,1,0:T(8,128)(2,1)S(1)}, u32[]{:S(2)}, u32[]{:S(2)}) async-start(bf16[4,128,1024]{2,1,0:T(8,128)(2,1)} %shard_map.43), calls=%async_computation.5 | async-start | bytes 2097152 | tf_op jit(solution)/shard_map/all_to_all | solution.py:200
  44.1 10.7 %psum.23 = f32[8,128]{1,0:T(8,128)S(1)} all-reduce(f32[8,128]{1,0:T(8,128)S(1)} %psum.22), channel_id=1, replica_groups=mesh['zh'=8,'zl'=2,'xh'=2,'y'=4,'core'=2,'xl'=2] {'y'}, use_global_device_ids=true, to_apply=%region_2.0 | all-reduce | flops 1024 | bytes 8192 | tf_op jit(solution)/shard_map/psum | solution.py:243
  54.8 2.0 %log_convert_fusion.expr_ref = bf16[768,1024]{1,0:T(8,128)(2,1)S(1)} fusion(bf16[768,1024]{1,0:T(8,128)(2,1)} %get-tuple-element.73, f32[768]{0:T(1024)S(1)} %divide_bitcast_fusion), kind=kLoop, calls=%fused_computation.54 | loop fusion | flops 3145728 | bytes 3148800 | tf_op jit(solution)/shard_map/convert_element_type | solution.py:247
  56.9 1.0 shard_map.44
  57.9 15.6 %all_to_all.36.block_ref = bf16[16,32,768]{2,1,0:T(8,128)(2,1)S(1)} all-to-all(bf16[16,32,768]{2,1,0:T(8,128)(2,1)S(1)} %bitcast.16), channel_id=1, replica_groups=mesh['zh'=8,'zl'=2,'xh'=2,'y'=4,'core'=2,'xl'=2] {'y','core','xl'}, dimensions={0} | all-to-all | bytes 1572864 | tf_op jit(solution)/shard_map/all_to_all | solution.py:252
  73.5 1.0 shard_map.45
  74.5 3.6 %all-to-all-start.7 = ((bf16[16,32,768]{2,1,0:T(8,128)(2,1)}), bf16[16,32,768]{2,1,0:T(8,128)(2,1)S(1)}, u32[]{:S(2)}, u32[]{:S(2)}) async-start(bf16[16,32,768]{2,1,0:T(8,128)(2,1)} %shard_map.45), calls=%async_computation.7 | async-start | bytes 1572864 | tf_op jit(solution)/shard_map/all_to_all | solution.py:200
  78.8 11.7 %all-to-all-done.7 = bf16[16,32,768]{2,1,0:T(8,128)(2,1)S(1)} async-done(((bf16[16,32,768]{2,1,0:T(8,128)(2,1)}), bf16[16,32,768]{2,1,0:T(8,128)(2,1)S(1)}, u32[]{:S(2)}, u32[]{:S(2)}) %all-to-all-start.7) | async-done | bytes 786464 | tf_op jit(solution)/shard_map/all_to_all | solution.py:200
  90.6 59.6 %conditional.1 = (f32[16,1024]{1,0:T(8,128)S(1)}, f32[]{:T(128)}) conditional(s32[]{:T(128)} %convert_element_type.34, (bf16[512,768]{1,0:T(8,128)(2,1)S(1)}, bf16[768,1024]{1,0:T(8,128)(2,1)S(1)}, f32[1,1024]{1,0:T(1,128)S(1)}, f32[1,128]{1,0:T(1,128)S(1)}, s32[]{:T(128)}, /*index=5*/s32[]{:T(128)}, s32[2]{0:T(128)S(1)}, ...), branch_computations={%region_4.0_spmd, %region_5.6_spmd} | conditional | flops 839332 | bytes 7313808 | solution.py:290
  90.6 2.5 %branch_1_fun.3 = bf16[4,128,1664]{2,1,0:T(8,128)(2,1)} custom-call(bf16[512,768]{1,0:T(8,128)(2,1)S(1)} %get-tuple-element.52.proj_ref, bf16[768,1024]{1,0:T(8,128)(2,1)S(1)} %get-tuple-element.53.expr_ref, f32[1,1024]{1,0:T(1,128)S(1)} %get-tuple-element.54.sums_ref, f32[1,128]{1,0:T(1,128)S(1)} %get-tuple-element.55.head_ref), custom_call_target="tpu_custom_call" | custom-call | tf_op jit(solution)/shard_map/cond/branch_1_fun/pallas_call | solution.py:267
  93.0 5.9 %all-to-all-start.2 = ((bf16[4,128,1664]{2,1,0:T(8,128)(2,1)}), bf16[4,128,1664]{2,1,0:T(8,128)(2,1)S(1)}, u32[]{:S(2)}, u32[]{:S(2)}) async-start(bf16[4,128,1664]{2,1,0:T(8,128)(2,1)} %branch_1_fun.3), calls=%async_computation.2 | async-start | bytes 3407872 | tf_op jit(solution)/shard_map/cond/branch_1_fun/all_to_all | solution.py:268
  99.0 19.0 %all-to-all-done.2.got_ref = bf16[4,128,1664]{2,1,0:T(8,128)(2,1)S(1)} async-done(((bf16[4,128,1664]{2,1,0:T(8,128)(2,1)}), bf16[4,128,1664]{2,1,0:T(8,128)(2,1)S(1)}, u32[]{:S(2)}, u32[]{:S(2)}) %all-to-all-start.2) | async-done | bytes 1703968 | tf_op jit(solution)/shard_map/cond/branch_1_fun/all_to_all | solution.py:268
  118.0 1.6 %branch_1_fun.4 = bf16[8,16,1792]{2,1,0:T(8,128)(2,1)} custom-call(bf16[4,128,1664]{2,1,0:T(8,128)(2,1)S(1)} %all-to-all-done.2.got_ref, bf16[128,512]{1,0:T(8,128)(2,1)S(1)} %get-tuple-element.77.refs_0_, bf16[128,512]{1,0:T(8,128)(2,1)S(1)} %get-tuple-element.78.refs_1_), custom_call_target="tpu_custom_call" | custom-call | tf_op jit(solution)/shard_map/cond/branch_1_fun/pallas_call | solution.py:274
  119.6 5.4 %all-to-all-start.3 = ((bf16[8,16,1792]{2,1,0:T(8,128)(2,1)}), bf16[8,16,1792]{2,1,0:T(8,128)(2,1)S(1)}, u32[]{:S(2)}, u32[]{:S(2)}) async-start(bf16[8,16,1792]{2,1,0:T(8,128)(2,1)} %branch_1_fun.4), calls=%async_computation.3 | async-start | bytes 917504 | tf_op jit(solution)/shard_map/cond/branch_1_fun/all_to_all | solution.py:275
  125.3 23.2 %all-to-all-done.3.got_ref = bf16[8,16,1792]{2,1,0:T(8,128)(2,1)S(1)} async-done(((bf16[8,16,1792]{2,1,0:T(8,128)(2,1)}), bf16[8,16,1792]{2,1,0:T(8,128)(2,1)S(1)}, u32[]{:S(2)}, u32[]{:S(2)}) %all-to-all-start.3) | async-done | bytes 458784 | tf_op jit(solution)/shard_map/cond/branch_1_fun/all_to_all | solution.py:275
  148.6 1.6 %branch_1_fun.5 = (f32[16,1024]{1,0:T(8,128)S(1)}, f32[1,1]{1,0:T(1,128)}) custom-call(s32[2]{0:T(128)S(1)} %get-tuple-element.51.place_ref, bf16[8,16,1792]{2,1,0:T(8,128)(2,1)S(1)} %all-to-all-done.3.got_ref, f32[16,1024]{1,0:T(8,128)S(1)} %get-tuple-element.57.coef_ref, bf16[16,512]{1,0:T(8,128)(2,1)S(1)} %get-tuple-element.79.refs_0_, ...), custom_call_target="tpu_custom_call" | custom-call | tf_op jit(solution)/shard_map/cond/branch_1_fun/pallas_call | solution.py:286
  150.2 0.6 copy-done.1
  (18 shorter events, 1.1 us)
Async XLA Ops:
  2.2 34.6 %all-to-all-start.4 = ((bf16[8,16,1024]{2,1,0:T(8,128)(2,1)}), bf16[8,16,1024]{2,1,0:T(8,128)(2,1)S(1)}, u32[]{:S(2)}, u32[]{:S(2)}) async-start(bf16[8,16,1024]{2,1,0:T(8,128)(2,1)} %shard_map.41), calls=%async_computation.4 | async-start | bytes 524288 | tf_op jit(solution)/shard_map/all_to_all | solution.py:200
  37.8 19.1 %all-to-all-start.5 = ((bf16[4,128,1024]{2,1,0:T(8,128)(2,1)}), bf16[4,128,1024]{2,1,0:T(8,128)(2,1)S(1)}, u32[]{:S(2)}, u32[]{:S(2)}) async-start(bf16[4,128,1024]{2,1,0:T(8,128)(2,1)} %shard_map.43), calls=%async_computation.5 | async-start | bytes 2097152 | tf_op jit(solution)/shard_map/all_to_all | solution.py:200
  74.5 16.0 %all-to-all-start.7 = ((bf16[16,32,768]{2,1,0:T(8,128)(2,1)}), bf16[16,32,768]{2,1,0:T(8,128)(2,1)S(1)}, u32[]{:S(2)}, u32[]{:S(2)}) async-start(bf16[16,32,768]{2,1,0:T(8,128)(2,1)} %shard_map.45), calls=%async_computation.7 | async-start | bytes 1572864 | tf_op jit(solution)/shard_map/all_to_all | solution.py:200
  78.2 12.4 %copy-start = (f32[1024,16]{0,1:T(8,128)S(1)}, f32[1024,16]{0,1:T(8,128)}, u32[]{:S(2)}) copy-start(f32[1024,16]{0,1:T(8,128)} %param.5) | copy-start | bytes 196612
  93.0 25.0 %all-to-all-start.2 = ((bf16[4,128,1664]{2,1,0:T(8,128)(2,1)}), bf16[4,128,1664]{2,1,0:T(8,128)(2,1)S(1)}, u32[]{:S(2)}, u32[]{:S(2)}) async-start(bf16[4,128,1664]{2,1,0:T(8,128)(2,1)} %branch_1_fun.3), calls=%async_computation.2 | async-start | bytes 3407872 | tf_op jit(solution)/shard_map/cond/branch_1_fun/all_to_all | solution.py:268
  119.6 29.0 %all-to-all-start.3 = ((bf16[8,16,1792]{2,1,0:T(8,128)(2,1)}), bf16[8,16,1792]{2,1,0:T(8,128)(2,1)S(1)}, u32[]{:S(2)}, u32[]{:S(2)}) async-start(bf16[8,16,1792]{2,1,0:T(8,128)(2,1)} %branch_1_fun.4), calls=%async_computation.3 | async-start | bytes 917504 | tf_op jit(solution)/shard_map/cond/branch_1_fun/all_to_all | solution.py:275
  150.2 0.6 copy-start.1
